TPU v7x, 32 devices: a whole 2x2x4 slice. The times are simulated.
32 devices in a mesh: rows: 8 (over z, x), heads: 4 (over y, core).
Axes of the slice: x: 2, y: 2, z: 4, core: 2. Of those that a mesh axis runs over, the one named last changes fastest.
Arguments:
- pair_rep: bfloat16 [12, 256, 256, 128], P(None, 'rows'), may hold values from -6 to 6
- lengths: int32 [12], replicated, may hold values from 64 to 256, as said below
- proj_weight: float32 [128, 512], P('rows', 'heads'), may hold values from -0.5 to 0.5
- bias_weight: float32 [128, 4], P('rows', 'heads'), may hold values from -0.5 to 0.5
- out_weight: float32 [128, 128], P('heads', 'rows'), may hold values from -3 to 3
- up_weight: float32 [128, 512], P(('rows', 'heads')), may hold values from -0.5 to 0.5
- down_weight: float32 [512, 128], P(('rows', 'heads')), may hold values from -0.25 to 0.25
- norm_gains: float32 [4, 128], P(None, ('rows', 'heads')), may hold values from -1 to 1.4, as said below
- proj_moment: float32 [128, 512], P('rows', 'heads'), may hold values from -256 to 256
- bias_moment: float32 [128, 4], P('rows', 'heads'), may hold values from -512 to 512
- out_moment: float32 [128, 128], P('heads', 'rows'), may hold values from -256 to 256
- up_moment: float32 [128, 512], P(('rows', 'heads')), may hold values from -2560 to 2560
- down_moment: float32 [512, 128], P(('rows', 'heads')), may hold values from -2560 to 2560
- gains_moment: float32 [4, 128], P(None, ('rows', 'heads')), may hold values from -5120 to 5120
- proj_average: float32 [128, 512], P('rows', 'heads'), may hold values from -0.5 to 0.5
- bias_average: float32 [128, 4], P('rows', 'heads'), may hold values from -0.5 to 0.5
- out_average: float32 [128, 128], P('heads', 'rows'), may hold values from -3 to 3
- up_average: float32 [128, 512], P(('rows', 'heads')), may hold values from -0.5 to 0.5
- down_average: float32 [512, 128], P(('rows', 'heads')), may hold values from -0.25 to 0.25
- gains_average: float32 [4, 128], P(None, ('rows', 'heads')), may hold values from 0.5 to 1.5
- cotangent: bfloat16 [12, 256, 256, 128], P(None, 'rows', 'heads'), may hold values from -6 to 6
Outputs:
- result: bfloat16 [12, 256, 256, 128], P(None, 'rows', 'heads')
- d_pair: bfloat16 [12, 256, 256, 128], P(None, 'rows', 'heads')
- new_proj: float32 [128, 512], P('rows', 'heads')
- new_bias: float32 [128, 4], P('rows', 'heads')
- new_out: float32 [128, 128], P('heads', 'rows')
- new_up: float32 [128, 512], P(('rows', 'heads'))
- new_down: float32 [512, 128], P(('rows', 'heads'))
- new_gains: float32 [4, 128], P(None, ('rows', 'heads'))
- proj_moment_new: float32 [128, 512], P('rows', 'heads')
- bias_moment_new: float32 [128, 4], P('rows', 'heads')
- out_moment_new: float32 [128, 128], P('heads', 'rows')
- up_moment_new: float32 [128, 512], P(('rows', 'heads'))
- down_moment_new: float32 [512, 128], P(('rows', 'heads'))
- gains_moment_new: float32 [4, 128], P(None, ('rows', 'heads'))
- proj_average_new: float32 [128, 512], P('rows', 'heads')
- bias_average_new: float32 [128, 4], P('rows', 'heads')
- out_average_new: float32 [128, 128], P('heads', 'rows')
- up_average_new: float32 [128, 512], P(('rows', 'heads'))
- down_average_new: float32 [512, 128], P(('rows', 'heads'))
- gains_average_new: float32 [4, 128], P(None, ('rows', 'heads'))
Inputs may be any that keep to these rules, and one draw needn't show every extreme that they name: `lengths`: each item's residues 0 to its length - 1 are real; one item has all 256. `norm_gains`: rows 0 and 2 are gains, rows 1 and 3 shifts.
All inputs are finite; a program needn't handle non-finite values.
Results may differ from a plain program's by a relative error of at most 0.025.
Values may be sent and summed in bfloat16 or wider, within the bound.
A program may use at most 576 MiB of HBM per device.

v0:
```python
import math

import jax
import jax.numpy as jnp
from jax import lax
from jax.sharding import PartitionSpec as P

EPSILON = 1e-05
MOMENTUM = 0.9
AVERAGE = 0.6
RATES = (0.5, 0.3, 3.0, 0.05, 0.03, 0.1)


def normalize(values):
    centre = jnp.mean(values, axis=-1, keepdims=True)
    shifted = values - centre
    spread = lax.rsqrt(jnp.mean(shifted * shifted, axis=-1, keepdims=True) + EPSILON)
    return (shifted * spread, spread)


def norm_back(d_hat, normal, spread):
    first = jnp.mean(d_hat, axis=-1, keepdims=True)
    second = jnp.mean(d_hat * normal, axis=-1, keepdims=True)
    return spread * (d_hat - first - normal * second)


def flat_product(left, right):
    return jnp.einsum(
        "na,nb->ab",
        left.reshape(-1, left.shape[-1]),
        right.reshape(-1, right.shape[-1]),
        preferred_element_type=jnp.float32,
    )


def scores_of(proj_item, bias_item, mask_item, head_width):
    query_part = proj_item[..., :head_width]
    key_part = proj_item[..., head_width : 2 * head_width]
    logits = jnp.einsum(
        "ijd,ikd->ijk", query_part, key_part, preferred_element_type=jnp.float32
    ) * (1.0 / math.sqrt(head_width))
    logits = logits + bias_item.astype(jnp.float32)[None]
    return jnp.where(mask_item[None, None, :], logits, -1000000000.0)


def update(weight, gradient, moment, average, step_rate, root_pairs):
    moment_next = MOMENTUM * moment + gradient
    weight_next = weight - step_rate / root_pairs * (gradient + MOMENTUM * moment_next)
    return (weight_next, moment_next, AVERAGE * average + (1.0 - AVERAGE) * weight_next)


def shards(
    pair_rep,
    lengths,
    proj_weight,
    bias_weight,
    out_weight,
    up_weight,
    down_weight,
    norm_gains,
    proj_moment,
    bias_moment,
    out_moment,
    up_moment,
    down_moment,
    gains_moment,
    proj_average,
    bias_average,
    out_average,
    up_average,
    down_average,
    gains_average,
    cotangent,
):
    low_type = jnp.bfloat16
    full_type = jnp.float32
    residues = pair_rep.shape[2]
    quarter = cotangent.shape[2]
    head_width = out_weight.shape[0]
    proj_all, bias_col, out_head = (
        lax.all_gather(proj_weight.astype(low_type), "rows", axis=0, tiled=True),
        lax.all_gather(bias_weight.astype(low_type), "rows", axis=0, tiled=True),
        lax.all_gather(out_weight.astype(low_type), "rows", axis=1, tiled=True),
    )
    up_all, down_all, gain_low = (
        lax.all_gather(up_weight.astype(low_type), ("rows", "heads"), axis=0, tiled=True),
        lax.all_gather(down_weight.astype(low_type), ("rows", "heads"), axis=0, tiled=True),
        lax.all_gather(norm_gains.astype(low_type), ("rows", "heads"), axis=1, tiled=True),
    )
    gain_vals = gain_low.astype(full_type)
    pair_wide = pair_rep.astype(full_type)
    normal_one, spread_one = normalize(pair_wide)
    normed = (normal_one * gain_vals[0] + gain_vals[1]).astype(low_type)
    projected = jnp.dot(normed, proj_all, preferred_element_type=full_type).astype(low_type)
    bias_part = jnp.dot(normed, bias_col, preferred_element_type=full_type)[..., 0].astype(low_type)
    bias_whole = lax.all_gather(bias_part, "rows", axis=1, tiled=True)
    key_mask = lax.broadcasted_iota(jnp.int32, (pair_rep.shape[0], residues), 1) < lengths[:, None]

    def attend(inputs):
        proj_item, bias_item, mask_item = inputs
        logits = scores_of(proj_item, bias_item, mask_item, head_width)
        row_peak = jnp.max(logits, axis=-1, keepdims=True)
        log_total = row_peak + jnp.log(jnp.sum(jnp.exp(logits - row_peak), axis=-1, keepdims=True))
        probs_low = jnp.exp(logits - log_total).astype(low_type)
        values = proj_item[..., 2 * head_width : 3 * head_width]
        blended = jnp.einsum("ijk,ikd->ijd", probs_low, values, preferred_element_type=full_type)
        gate_open = jax.nn.sigmoid(proj_item[..., 3 * head_width :].astype(full_type))
        return ((gate_open * blended).astype(low_type), blended, log_total[..., 0])

    gated_out, blended_all, totals_all = lax.map(attend, (projected, bias_whole, key_mask))
    head_index = lax.axis_index("heads")
    pair_quarter = lax.dynamic_slice_in_dim(pair_wide, head_index * quarter, quarter, 2)
    head_term = jnp.dot(gated_out, out_head, preferred_element_type=full_type)
    branch_sum = lax.psum_scatter(
        head_term.astype(jnp.bfloat16), "heads", scatter_dimension=2, tiled=True
    ).astype(jnp.float32)
    middle = pair_quarter + branch_sum
    normal_two, spread_two = normalize(middle)
    shaped = (normal_two * gain_vals[2] + gain_vals[3]).astype(low_type)
    hidden_pre = jnp.dot(shaped, up_all, preferred_element_type=full_type)
    hidden = jax.nn.silu(hidden_pre).astype(low_type)
    result = (middle + jnp.dot(hidden, down_all, preferred_element_type=full_type)).astype(low_type)
    cot_wide = cotangent.astype(full_type)
    d_hidden = jnp.einsum("abjc,hc->abjh", cotangent, down_all, preferred_element_type=full_type)
    sigmoid_pre = jax.nn.sigmoid(hidden_pre)
    d_pre = (d_hidden * sigmoid_pre * (1.0 + hidden_pre * (1.0 - sigmoid_pre))).astype(low_type)
    grad_down = flat_product(hidden, cotangent)
    grad_up = flat_product(shaped, d_pre)
    d_shaped = jnp.einsum("abjh,ch->abjc", d_pre, up_all, preferred_element_type=full_type)
    gain_two = jnp.sum(d_shaped * normal_two, axis=(0, 1, 2))
    shift_two = jnp.sum(d_shaped, axis=(0, 1, 2))
    d_middle = cot_wide + norm_back(d_shaped * gain_vals[2], normal_two, spread_two)
    d_middle_low = d_middle.astype(low_type)
    d_rows = lax.all_gather(d_middle_low, "heads", axis=2, tiled=True)
    d_gated = jnp.einsum(
        "abjc,dc->abjd", d_rows, out_head, preferred_element_type=full_type
    ).astype(low_type)
    grad_out = flat_product(gated_out, d_rows)

    def attend_back(inputs):
        proj_item, bias_item, mask_item, total_item, blend_item, d_low = inputs
        d_item = d_low.astype(full_type)
        logits = scores_of(proj_item, bias_item, mask_item, head_width)
        probs_full = jnp.exp(logits - total_item[..., None])
        query_part = proj_item[..., :head_width]
        key_part = proj_item[..., head_width : 2 * head_width]
        values = proj_item[..., 2 * head_width : 3 * head_width]
        gate_open = jax.nn.sigmoid(proj_item[..., 3 * head_width :].astype(full_type))
        d_blend = (d_item * gate_open).astype(low_type)
        d_gate = d_item * blend_item * gate_open * (1.0 - gate_open)
        d_values = jnp.einsum(
            "ijk,ijd->ikd", probs_full.astype(low_type), d_blend, preferred_element_type=full_type
        )
        d_probs = jnp.einsum("ijd,ikd->ijk", d_blend, values, preferred_element_type=full_type)
        d_logits = (
            probs_full * (d_probs - jnp.sum(probs_full * d_probs, axis=-1, keepdims=True))
        ).astype(low_type)
        score_scale = 1.0 / math.sqrt(head_width)
        d_query = (
            jnp.einsum("ijk,ikd->ijd", d_logits, key_part, preferred_element_type=full_type)
            * score_scale
        )
        d_keys = (
            jnp.einsum("ijk,ijd->ikd", d_logits, query_part, preferred_element_type=full_type)
            * score_scale
        )
        d_bias_item = jnp.sum(d_logits, axis=0, dtype=full_type)
        d_proj_item = jnp.concatenate([d_query, d_keys, d_values, d_gate], axis=-1).astype(low_type)
        return (d_proj_item, d_bias_item)

    d_projected, d_bias_rows = lax.map(
        attend_back, (projected, bias_whole, key_mask, totals_all, blended_all, d_gated)
    )
    d_bias = (
        lax.psum_scatter(d_bias_rows.astype(jnp.bfloat16), "rows", scatter_dimension=1, tiled=True)
        .astype(jnp.float32)
        .astype(low_type)
    )
    bias_row = bias_col[:, 0].astype(full_type)
    d_normed = jnp.einsum("abjk,ck->abjc", d_projected, proj_all, preferred_element_type=full_type)
    d_normed = d_normed + d_bias.astype(full_type)[..., None] * bias_row
    grad_proj = flat_product(normed, d_projected)
    grad_bias = flat_product(normed, d_bias[..., None])
    d_norm_quarter = lax.psum_scatter(
        d_normed.astype(jnp.bfloat16), "heads", scatter_dimension=2, tiled=True
    ).astype(jnp.float32)
    normal_three, spread_three = normalize(pair_quarter)
    d_pair = (
        d_middle + norm_back(d_norm_quarter * gain_vals[0], normal_three, spread_three)
    ).astype(low_type)
    gain_grads = jnp.stack(
        [
            jnp.sum(d_norm_quarter * normal_three, axis=(0, 1, 2)),
            jnp.sum(d_norm_quarter, axis=(0, 1, 2)),
            gain_two,
            shift_two,
        ]
    )
    sum_proj, sum_bias, sum_out = (
        lax.psum_scatter(
            grad_proj.astype(jnp.bfloat16), "rows", scatter_dimension=0, tiled=True
        ).astype(jnp.float32),
        lax.psum_scatter(
            grad_bias.astype(jnp.bfloat16), "rows", scatter_dimension=0, tiled=True
        ).astype(jnp.float32),
        lax.psum_scatter(
            grad_out.astype(jnp.bfloat16), "rows", scatter_dimension=1, tiled=True
        ).astype(jnp.float32),
    )
    sum_up, sum_down, sum_gains = (
        lax.psum_scatter(grad_up, ("rows", "heads"), scatter_dimension=0, tiled=True),
        lax.psum_scatter(grad_down, ("rows", "heads"), scatter_dimension=0, tiled=True),
        lax.psum_scatter(gain_grads, ("rows", "heads"), scatter_dimension=1, tiled=True),
    )
    root_pairs = math.sqrt(pair_rep.shape[0] * residues * residues)
    proj_next = update(proj_weight, sum_proj, proj_moment, proj_average, RATES[0], root_pairs)
    bias_next = update(bias_weight, sum_bias, bias_moment, bias_average, RATES[1], root_pairs)
    out_next = update(out_weight, sum_out, out_moment, out_average, RATES[2], root_pairs)
    up_next = update(up_weight, sum_up, up_moment, up_average, RATES[3], root_pairs)
    down_next = update(down_weight, sum_down, down_moment, down_average, RATES[4], root_pairs)
    gains_next = update(norm_gains, sum_gains, gains_moment, gains_average, RATES[5], root_pairs)
    return (
        result,
        d_pair,
        proj_next[0],
        bias_next[0],
        out_next[0],
        up_next[0],
        down_next[0],
        gains_next[0],
        proj_next[1],
        bias_next[1],
        out_next[1],
        up_next[1],
        down_next[1],
        gains_next[1],
        proj_next[2],
        bias_next[2],
        out_next[2],
        up_next[2],
        down_next[2],
        gains_next[2],
    )


def solution(mesh):
    in_specs = (
        P(None, "rows", None, None),
        P(),
        P("rows", "heads"),
        P("rows", "heads"),
        P("heads", "rows"),
        P(("rows", "heads"), None),
        P(("rows", "heads"), None),
        P(None, ("rows", "heads")),
        P("rows", "heads"),
        P("rows", "heads"),
        P("heads", "rows"),
        P(("rows", "heads"), None),
        P(("rows", "heads"), None),
        P(None, ("rows", "heads")),
        P("rows", "heads"),
        P("rows", "heads"),
        P("heads", "rows"),
        P(("rows", "heads"), None),
        P(("rows", "heads"), None),
        P(None, ("rows", "heads")),
        P(None, "rows", "heads", None),
    )
    out_specs = (
        P(None, "rows", "heads", None),
        P(None, "rows", "heads", None),
        P("rows", "heads"),
        P("rows", "heads"),
        P("heads", "rows"),
        P(("rows", "heads"), None),
        P(("rows", "heads"), None),
        P(None, ("rows", "heads")),
        P("rows", "heads"),
        P("rows", "heads"),
        P("heads", "rows"),
        P(("rows", "heads"), None),
        P(("rows", "heads"), None),
        P(None, ("rows", "heads")),
        P("rows", "heads"),
        P("rows", "heads"),
        P("heads", "rows"),
        P(("rows", "heads"), None),
        P(("rows", "heads"), None),
        P(None, ("rows", "heads")),
    )
    return jax.shard_map(shards, mesh=mesh, in_specs=in_specs, out_specs=out_specs, check_vma=False)
```

profile of v0, /device:TPU:0, one launch (start us, length us, event | category | flops | bytes accessed | tf_op | source)
XLA Modules:
  0.0 2226.5 jit_solution(14865666137313451443)
XLA Ops:
  10.0 23.1 %all-reduce = bf16[128]{0:T(256)(128)(2,1)S(1)} all-reduce(bf16[128]{0:T(256)(128)(2,1)S(1)} %dynamic-update-slice), channel_id=1, replica_groups=mesh['rows'=8,'heads'=4] {'rows'}, use_global_device_ids=true, to_apply=%add | all-reduce | flops 128 | bytes 512 | tf_op jit(solution)/shard_map/reshape.4
  33.9 37.8 %all-gather = bf16[32,4,4]{2,1,0:T(4,128)(2,1)S(1)} all-gather(bf16[1,4,4]{2,1,0:T(4,128)(2,1)S(1)} %bitcast.197), channel_id=1, replica_groups=mesh['rows'=8,'heads'=4] {'rows','heads'}, dimensions={0}, use_global_device_ids=true | all-gather | bytes 1056 | tf_op jit(solution)/shard_map/all_gather | solution.py:88
  88.5 29.6 %multiply_reduce_fusion.1 = f32[12,32,256]{2,1,0:T(8,128)S(1)} fusion(bf16[12,32,256,128]{3,2,1,0:T(8,128)(2,1)S(1)} %copy-done.3, f32[12,32,256]{2,1,0:T(8,128)S(1)} %broadcast_multiply_fusion), kind=kLoop, calls=%fused_computation.59 | loop fusion | flops 50233344 | bytes 25952256 | tf_op jit(solution)/shard_map/reduce_sum | solution.py:17
  118.2 38.1 %fusion.62 = bf16[1,12,32,256]{3,0,2,1:T(2,128)(2,1)S(1)} fusion(bf16[128]{0:T(256)(128)(2,1)S(1)} %all-reduce, bf16[12,32,256,128]{3,2,1,0:T(8,128)(2,1)S(1)} %copy-done.3, f32[128]{0:T(128)S(1)} %get-tuple-element.250, f32[128]{0:T(128)S(1)} %get-tuple-element.251, f32[12,32,256]{2,1,0:T(8,128)S(1)} %add_rsqrt_fusion, ...), kind=kOutput, calls=%fused_computation.143 | convolution fusion | flops 100663296 | bytes 26150144 | tf_op jit(solution)/shard_map/dot_general | solution.py:95
  157.2 30.5 %all_gather.25 = bf16[128,128]{1,0:T(8,128)(2,1)S(1)} all-gather(bf16[16,128]{1,0:T(8,128)(2,1)S(1)} %convert_element_type.151), channel_id=1, replica_groups=mesh['rows'=8,'heads'=4] {'rows'}, dimensions={0}, use_global_device_ids=true | all-gather | bytes 36864 | tf_op jit(solution)/shard_map/all_gather | solution.py:81
  187.6 35.4 %convolution_convert_fusion = bf16[12,32,256,128]{3,2,1,0:T(8,128)(2,1)} fusion(bf16[128,128]{1,0:T(8,128)(2,1)S(1)} %all_gather.25, bf16[12,32,256,128]{3,2,1,0:T(8,128)(2,1)} %param.25, f32[128]{0:T(128)S(1)} %get-tuple-element.250, f32[128]{0:T(128)S(1)} %get-tuple-element.251, f32[12,32,256]{2,1,0:T(8,128)S(1)} %add_rsqrt_fusion, ...), kind=kOutput, calls=%fused_computation.67 | convolution fusion | flops 3309305856 | bytes 51151872 | tf_op jit(solution)/shard_map/dot_general | solution.py:94
  223.1 32.7 %copy.87 = bf16[12,32,256,128]{2,3,1,0:T(8,128)(2,1)} copy(bf16[12,32,256,128]{3,2,1,0:T(8,128)(2,1)} %convolution_convert_fusion) | data formatting | bytes 50331648 | tf_op jit(solution)/shard_map/while | solution.py:110
  255.8 30.6 %all_gather.28 = bf16[32,128]{0,1:T(8,128)(2,1)S(1)} all-gather(bf16[32,16]{0,1:T(8,128)(2,1)S(1)} %convert_element_type.155), channel_id=1, replica_groups=mesh['rows'=8,'heads'=4] {'rows'}, dimensions={1}, use_global_device_ids=true | all-gather | bytes 9216 | tf_op jit(solution)/shard_map/all_gather | solution.py:83
  289.1 140.4 %while.26 = (s32[]{:T(128)}, bf16[12,32,256,32]{2,3,1,0:T(8,128)(2,1)}, f32[12,32,256,32]{2,3,1,0:T(8,128)}, f32[12,32,256]{2,1,0:T(8,128)}, bf16[12,32,256,128]...) while((s32[]{:T(128)}, ...), condition=%wide.region_5.6_spmd, body=%wide.region_2.5_spmd.sunk | while | flops 299425792 | bytes 36570996 | solution.py:110
  443.1 31.2 %convert_element_type.147 = f32[12,32,256,128]{3,2,1,0:T(8,128)} convert(bf16[12,32,256,128]{3,2,1,0:T(8,128)(2,1)} %param.25) | non-fusion elementwise | flops 12582912 | bytes 75497472 | tf_op jit(solution)/shard_map/convert_element_type | solution.py:91
  474.4 38.1 %all-gather.1 = bf16[32,4,512]{2,1,0:T(4,128)(2,1)S(1)} all-gather(bf16[1,4,512]{2,1,0:T(4,128)(2,1)S(1)} %convert_bitcast_fusion), channel_id=1, replica_groups=mesh['rows'=8,'heads'=4] {'rows','heads'}, dimensions={0}, use_global_device_ids=true | all-gather | bytes 135168 | tf_op jit(solution)/shard_map/all_gather | solution.py:86
  520.5 100.5 %reduce-scatter.11.cloned.1.call-done = bf16[12,32,64,128]{3,2,1,0:T(8,128)(2,1)} async-done(((bf16[12,32,256,128]{3,2,1,0:T(8,128)(2,1)}), bf16[12,32,64,128]{3,2,1,0:T(8,128)(2,1)}) %reduce-scatter.11.cloned.1.call-update) | async-done | bytes 6291472 | tf_op jit(solution)/shard_map/reduce_scatter | solution.py:114
  641.9 24.6 %multiply_convert_fusion.3 = (bf16[12,32,64,512]{3,2,1,0:T(8,128)(2,1)}, f32[12,32,64,512]{3,2,1,0:T(8,128)}) fusion(bf16[128,512,1,1]{1,0,2,3:T(8,128)(2,1)S(1)} %reshape.234, f32[12,32,64,128]{3,2,1,0:T(8,128)S(1)} %get-tuple-element.239, f32[128]{0:T(128)S(1)} %copy-done.29, f32[128]{0:T(128)S(1)} %copy-done.28, f32[12,32,64]{2,1,0:T(8,128)S(1)} %add_rsqrt_fusion.2, ...), kind=kOutput, calls=%fused_computation.56 | convolution fusion | flops 3299868672 | bytes 88409088 | tf_op jit(solution)/shard_map/dot_general | solution.py:120
  679.0 133.5 %reduce-scatter.21.cloned.1.call-done = f32[16,128]{1,0:T(8,128)} async-done(((f32[512,128]{1,0:T(8,128)}), f32[16,128]{1,0:T(8,128)}) %reduce-scatter.21.cloned.1.call-update) | async-done | bytes 8208 | tf_op jit(solution)/shard_map/reduce_scatter | solution.py:212
  813.8 37.1 %all_gather.30 = bf16[512,128]{1,0:T(8,128)(2,1)S(1)} all-gather(bf16[16,128]{1,0:T(8,128)(2,1)S(1)} %get-tuple-element.247), channel_id=1, replica_groups=mesh['rows'=8,'heads'=4] {'rows','heads'}, dimensions={0}, use_global_device_ids=true | all-gather | bytes 135168 | tf_op jit(solution)/shard_map/all_gather | solution.py:87
  850.9 34.1 %multiply_convert_fusion.2 = bf16[12,32,64,512]{3,2,1,0:T(8,128)(2,1)} fusion(f32[12,32,64,512]{3,2,1,0:T(8,128)} %get-tuple-element.253, bf16[12,32,64,128]{3,2,1,0:T(8,128)(2,1)} %param.45, bf16[512,128]{1,0:T(8,128)(2,1)S(1)} %all_gather.30), kind=kOutput, calls=%fused_computation.55 | convolution fusion | flops 3334471680 | bytes 81920000 | tf_op jit(solution)/shard_map/abjc,hc->abjh/dot_general | solution.py:124
  885.0 21.3 multiply_reduce_fusion.2
  910.9 16.7 fusion.64
  927.9 152.5 %all-gather.7.cloned.1.call-done = bf16[12,32,256,128]{3,2,1,0:T(8,128)(2,1)} async-done(((bf16[12,32,64,128]{3,2,1,0:T(8,128)(2,1)}), bf16[12,32,256,128]{3,2,1,0:T(8,128)(2,1)}) %all-gather.7.cloned.1.call-update) | async-done | bytes 25165840 | tf_op jit(solution)/shard_map/all_gather | solution.py:134
  1095.6 482.4 %while.27 = (s32[]{:T(128)}, bf16[12,32,256,128]{2,3,1,0:T(8,128)(2,1)}, bf16[12,256,256]{2,1,0:T(8,128)(2,1)}, pred[12,256]{1,0:T(8,128)(4,1)}, bf16[12,32,256,...) while((s32[]{:T(128)}, ...), condition=%wide.region_16.17_spmd, body=%wide.region_13.16_spmd.sunk | while | flops 712237056 | bytes 115246248 | solution.py:171
  1581.7 18.7 convolution_bitcast_fusion.1
  1616.6 43.9 %fusion.43 = bf16[128,128]{1,0:T(8,128)(2,1)} fusion(bf16[12,32,256,128]{2,3,1,0:T(8,128)(2,1)} %get-tuple-element.110, bf16[12,32,256,128]{3,2,1,0:T(8,128)(2,1)} %param.25, f32[128]{0:T(128)S(1)} %copy-done.57, f32[128]{0:T(128)S(1)} %copy-done.49, f32[12,32,256]{2,1,0:T(8,128)S(1)} %copy-done.22, f32[12,32,256]{2,1,0:T(8,128)S(1)} %copy-done.17), kind=kOutput, calls=%fused_computation.92 | convolution fusion | flops 3296739328 | bytes 51151872 | tf_op jit(solution)/shard_map/na,nb->ab/dot_general | solution.py:28
  1660.7 33.3 %fusion.46 = bf16[128,1]{0,1:T(2,128)(2,1)S(1)} fusion(bf16[12,32,256,1]{2,0,1,3:T(8,128)(2,1)} %bitcast.194, bf16[12,32,256,128]{3,2,1,0:T(8,128)(2,1)} %param.25, f32[128]{0:T(128)S(1)} %copy-done.57, f32[128]{0:T(128)S(1)} %copy-done.49, f32[12,32,256]{2,1,0:T(8,128)S(1)} %copy-done.22, f32[12,32,256]{2,1,0:T(8,128)S(1)} %copy-done.17), kind=kOutput, calls=%fused_computation.96 | convolution fusion | flops 100663424 | bytes 26150144 | tf_op jit(solution)/shard_map/na,nb->ab/dot_general | solution.py:28
  1694.9 23.8 %add_convert_fusion = bf16[12,32,256,128]{3,2,1,0:T(8,128)(2,1)} fusion(f32[128]{0:T(128)S(1)} %convert_element_type.169, f32[12,32,256]{2,1,0:T(8,128)S(1)} %copy_convert_fusion, bf16[12,32,256,128]{2,3,1,0:T(8,128)(2,1)} %get-tuple-element.110, bf16[128,128]{1,0:T(8,128)(2,1)S(1)} %copy-done.27), kind=kOutput, calls=%fused_computation.54 | convolution fusion | flops 3258974208 | bytes 50758144 | tf_op jit(solution)/shard_map/abjk,ck->abjc/dot_general | solution.py:180
  1719.7 18.2 add_convert_fusion.2
  1738.1 41.1 %all-reduce.5.cloned.1.call-done = f32[128,512]{1,0:T(8,128)} async-done(((f32[128,512]{1,0:T(8,128)}), f32[128,512]{1,0:T(8,128)}) %all-reduce.5.cloned.1.call-update) | async-done | bytes 262160
  1780.5 54.3 %reduce-scatter.19.cloned.1.call-done = bf16[32,16]{0,1:T(8,128)(2,1)} async-done(((bf16[32,128]{0,1:T(8,128)(2,1)}), bf16[32,16]{0,1:T(8,128)(2,1)}) %reduce-scatter.19.cloned.1.call-update) | async-done | bytes 1040 | tf_op jit(solution)/shard_map/reduce_scatter | solution.py:206
  1836.2 55.0 %reduce-scatter.17.cloned.1.call-done = bf16[16,128]{1,0:T(8,128)(2,1)} async-done(((bf16[128,128]{1,0:T(8,128)(2,1)}), bf16[16,128]{1,0:T(8,128)(2,1)}) %reduce-scatter.17.cloned.1.call-update) | async-done | bytes 4112 | tf_op jit(solution)/shard_map/reduce_scatter | solution.py:200
  1892.5 54.5 %reduce-scatter.23.cloned.1.call-done = bf16[16,1]{1,0:T(8,128)(2,1)} async-done(((bf16[128,1]{1,0:T(8,128)(2,1)}), bf16[16,1]{1,0:T(8,128)(2,1)}) %reduce-scatter.23.cloned.1.call-update) | async-done | bytes 48
  1948.3 180.6 %reduce-scatter.15.cloned.1.call-done = bf16[12,32,64,128]{3,2,1,0:T(8,128)(2,1)} async-done(((bf16[12,32,256,128]{3,2,1,0:T(8,128)(2,1)}), bf16[12,32,64,128]{3,2,1,0:T(8,128)(2,1)}) %reduce-scatter.15.cloned.1.call-update) | async-done | bytes 6291472 | tf_op jit(solution)/shard_map/reduce_scatter | solution.py:184
  2145.6 39.4 %all-reduce.2 = f32[4,128]{1,0:T(4,128)S(1)} all-reduce(f32[4,128]{1,0:T(4,128)S(1)} %pad_maximum_fusion), channel_id=10, replica_groups=mesh['rows'=8,'heads'=4] {'rows','heads'}, use_global_device_ids=true, to_apply=%region_30.31.clone | all-reduce | flops 512 | bytes 4096
  2185.7 33.7 %fusion.40 = bf16[12,32,64,128]{3,2,1,0:T(8,128)(2,1)} fusion(bf16[12,32,64,128]{3,2,1,0:T(8,128)(2,1)} %reduce-scatter.15.cloned.1.call-done, f32[12,32,256,128]{3,2,1,0:T(8,128)} %convert_element_type.147, s32[]{:T(128)S(6)} %select_n.10, f32[12,32,64]{2,1,0:T(8,128)S(1)} %broadcast_multiply_fusion.1, f32[12,32,64]{2,1,0:T(8,128)S(1)} %broadcast_multiply_fusion.2, ...), kind=kLoop, calls=%fused_computation.72 | loop fusion | flops 59768832 | bytes 57410564 | tf_op jit(solution)/shard_map/convert_element_type | solution.py:190
  (487 shorter events, 765.6 us)
Async XLA Ops:
  7.2 279.3 %all-gather.5.cloned.1.call-start = ((), (), s32[]{:S(2)}) async-start(), calls=%async_computation.7 | async-start | bytes 1769472 | tf_op jit(solution)/shard_map/all_gather | solution.py:96
  157.0 464.0 %reduce-scatter.11.cloned.1.call-start = ((), (), s32[]{:S(2)}) async-start(), calls=%async_computation.8 | async-start | bytes 31457280 | tf_op jit(solution)/shard_map/reduce_scatter | solution.py:114
  443.1 369.4 %reduce-scatter.21.cloned.1.call-start = ((), (), s32[]{:S(2)}) async-start(), calls=%async_computation.14 | async-start | bytes 270336 | tf_op jit(solution)/shard_map/reduce_scatter | solution.py:212
  634.3 272.0 %copy-start.6 = (f32[12,32,64]{2,1,0:T(8,128)}, f32[12,32,64]{2,1,0:T(8,128)S(1)}, u32[]{:S(2)}) copy-start(f32[12,32,64]{2,1,0:T(8,128)S(1)} %broadcast_multiply_fusion.6) | copy-start | bytes 294916
  641.8 264.6 %copy-start.10 = (f32[12,32,64]{2,1,0:T(8,128)}, f32[12,32,64]{2,1,0:T(8,128)S(1)}, u32[]{:S(2)}) copy-start(f32[12,32,64]{2,1,0:T(8,128)S(1)} %add_rsqrt_fusion.2) | copy-start | bytes 294916
  666.4 146.1 %copy-start.38 = (f32[16,128]{1,0:T(8,128)S(1)}, f32[16,128]{1,0:T(8,128)}, u32[]{:S(2)}) copy-start(f32[16,128]{1,0:T(8,128)} %param.43) | copy-start | bytes 24580
  679.0 401.5 %all-gather.7.cloned.1.call-start = ((), (), s32[]{:S(2)}) async-start(), calls=%async_computation.9 | async-start | bytes 31457280 | tf_op jit(solution)/shard_map/all_gather | solution.py:134
  910.9 169.5 %copy-start.24 = (bf16[32,128]{0,1:T(8,128)(2,1)S(1)}, bf16[32,128]{0,1:T(8,128)(2,1)}, u32[]{:S(2)}) copy-start(bf16[32,128]{0,1:T(8,128)(2,1)} %copy-done.23) | copy-start | bytes 24580
  927.7 733.0 %reduce-scatter.13.cloned.1.call-start = ((), (), s32[]{:S(2)}) async-start(), calls=%async_computation.10 | async-start | bytes 2359296 | tf_op jit(solution)/shard_map/reduce_scatter | solution.py:175
  1095.6 486.1 %copy-start.61 = (bf16[128]{0:T(256)(128)(2,1)S(1)}, bf16[128]{0:T(256)(128)(2,1)}, u32[]{:S(2)}) copy-start(bf16[128]{0:T(256)(128)(2,1)} %copy-done.60) | copy-start | bytes 772
  1095.6 486.1 %copy-start.30 = (f32[128]{0:T(128)S(1)}, f32[128]{0:T(128)}, u32[]{:S(2)}) copy-start(f32[128]{0:T(128)} %get-tuple-element.249) | copy-start | bytes 1540
  1581.7 197.5 %all-reduce.5.cloned.1.call-start = ((), (), s32[]{:S(2)}) async-start(), calls=%async_computation.16 | async-start | bytes 524288
  1600.5 234.4 %reduce-scatter.19.cloned.1.call-start = ((), (), s32[]{:S(2)}) async-start(), calls=%async_computation.13 | async-start | bytes 36864 | tf_op jit(solution)/shard_map/reduce_scatter | solution.py:206
  1616.5 274.7 %reduce-scatter.17.cloned.1.call-start = ((), (), s32[]{:S(2)}) async-start(), calls=%async_computation.12 | async-start | bytes 36864 | tf_op jit(solution)/shard_map/reduce_scatter | solution.py:200
  1660.6 286.4 %reduce-scatter.23.cloned.1.call-start = ((), (), s32[]{:S(2)}) async-start(), calls=%async_computation.15 | async-start | bytes 36864
  1694.7 434.2 %reduce-scatter.15.cloned.1.call-start = ((), (), s32[]{:S(2)}) async-start(), calls=%async_computation.11 | async-start | bytes 31457280 | tf_op jit(solution)/shard_map/reduce_scatter | solution.py:184
  1719.7 171.5 %copy-start.37 = (f32[16,128]{1,0:T(8,128)S(1)}, f32[16,128]{1,0:T(8,128)}, u32[]{:S(2)}) copy-start(f32[16,128]{1,0:T(8,128)} %param.27) | copy-start | bytes 24580
  1719.7 171.5 %copy-start.45 = (f32[16,128]{1,0:T(8,128)S(1)}, f32[16,128]{1,0:T(8,128)}, u32[]{:S(2)}) copy-start(f32[16,128]{1,0:T(8,128)} %param.39) | copy-start | bytes 24580
  1719.7 171.5 %copy-start.46 = (f32[16,128]{1,0:T(8,128)S(1)}, f32[16,128]{1,0:T(8,128)}, u32[]{:S(2)}) copy-start(f32[16,128]{1,0:T(8,128)} %param.33) | copy-start | bytes 24580
  1719.7 228.0 %copy-start.53 = (f32[16,1]{0,1:T(1,128)S(1)}, f32[16,1]{0,1:T(1,128)}, u32[]{:S(2)}) copy-start(f32[16,1]{0,1:T(1,128)} %param.28) | copy-start | bytes 196
  1719.7 228.0 %copy-start.54 = (f32[16,1]{0,1:T(1,128)S(1)}, f32[16,1]{0,1:T(1,128)}, u32[]{:S(2)}) copy-start(f32[16,1]{0,1:T(1,128)} %param.40) | copy-start | bytes 196
  1719.7 228.0 %copy-start.55 = (f32[16,1]{0,1:T(1,128)S(1)}, f32[16,1]{0,1:T(1,128)}, u32[]{:S(2)}) copy-start(f32[16,1]{0,1:T(1,128)} %param.34) | copy-start | bytes 196
  1719.7 409.2 %copy-start.9 = (f32[12,32,64]{2,1,0:T(8,128)S(1)}, f32[12,32,64]{2,1,0:T(8,128)}, u32[]{:S(2)}) copy-start(f32[12,32,64]{2,1,0:T(8,128)} %copy-done.8) | copy-start | bytes 294916
  1738.0 407.6 %copy-start.58 = (f32[128]{0:T(128)S(1)}, f32[128]{0:T(128)}, u32[]{:S(2)}) copy-start(f32[128]{0:T(128)} %get-tuple-element.178) | copy-start | bytes 1540
  1738.0 407.6 %copy-start.59 = (f32[128]{0:T(128)S(1)}, f32[128]{0:T(128)}, u32[]{:S(2)}) copy-start(f32[128]{0:T(128)} %get-tuple-element.181) | copy-start | bytes 1540
  1738.0 447.0 %copy-start.47 = (f32[4,4]{1,0:T(4,128)S(1)}, f32[4,4]{1,0:T(4,128)}, u32[]{:S(2)}) copy-start(f32[4,4]{1,0:T(4,128)} %param.32) | copy-start | bytes 196
  1738.0 447.0 %copy-start.50 = (f32[4,4]{1,0:T(4,128)S(1)}, f32[4,4]{1,0:T(4,128)}, u32[]{:S(2)}) copy-start(f32[4,4]{1,0:T(4,128)} %param.44) | copy-start | bytes 196
  1738.0 447.0 %copy-start.51 = (f32[4,4]{1,0:T(4,128)S(1)}, f32[4,4]{1,0:T(4,128)}, u32[]{:S(2)}) copy-start(f32[4,4]{1,0:T(4,128)} %param.38) | copy-start | bytes 196
  1738.0 447.7 %copy-start.7 = (f32[12,32,64]{2,1,0:T(8,128)S(1)}, f32[12,32,64]{2,1,0:T(8,128)}, u32[]{:S(2)}) copy-start(f32[12,32,64]{2,1,0:T(8,128)} %copy-done.6) | copy-start | bytes 294916
  1738.0 447.7 %copy-start.11 = (f32[12,32,64]{2,1,0:T(8,128)S(1)}, f32[12,32,64]{2,1,0:T(8,128)}, u32[]{:S(2)}) copy-start(f32[12,32,64]{2,1,0:T(8,128)} %copy-done.10) | copy-start | bytes 294916
  1738.0 447.7 %copy-start.13 = (f32[12,32,64]{2,1,0:T(8,128)S(1)}, f32[12,32,64]{2,1,0:T(8,128)}, u32[]{:S(2)}) copy-start(f32[12,32,64]{2,1,0:T(8,128)} %copy-done.12) | copy-start | bytes 294916
  1738.0 447.7 %copy-start.15 = (f32[12,32,64]{2,1,0:T(8,128)S(1)}, f32[12,32,64]{2,1,0:T(8,128)}, u32[]{:S(2)}) copy-start(f32[12,32,64]{2,1,0:T(8,128)} %copy-done.14) | copy-start | bytes 294916
  (53 other events, 2172.1 us)
Sparse Core Ops, SparseCore 0:
  157.2 40.3 all-gather.4
  443.2 177.7 reduce-scatter.10
  679.1 133.3 reduce-scatter.20
  927.8 152.5 all-gather.6
  1581.8 67.7 reduce-scatter.12
  1654.9 124.1 all-reduce.4
  1782.3 52.5 reduce-scatter.18
  1838.6 52.5 reduce-scatter.16
  1894.3 52.5 reduce-scatter.22
  1949.4 179.4 reduce-scatter.14
where the time goes:
time: 2240 us; the launch traced here: 2230 us
  waiting for transfers between devices  772 us (34%)
  matrix products  639 us (29%)
  other arithmetic  391 us (17%)
  blocking collectives  236 us (11%)
  local copies, waits for them, and re-layouts  169 us (8%)
    reduce_scatter x1, waiting for transfers between devices, shards(): lax.psum_scatter(d_normed.astype(jnp.bfloat16), 'heads', scatter_dimensio...  181 us
    all_gather x1, waiting for transfers between devices, shards(): d_rows = lax.all_gather(d_middle_low, 'heads', axis=2, tiled=True)  152 us
    reduce_scatter x1, waiting for transfers between devices, shards(): lax.psum_scatter(grad_down, ('rows', 'heads'), scatter_dimension=0, tiled...  133 us
    dot_general x5, matrix products, flat_product(): jnp.einsum('na,nb->ab', left.reshape(-1, left.shape[-1]), right.reshape(-...  124 us
    reduce_sum x12, other arithmetic, attend_back(): d_bias_item = jnp.sum(d_logits, axis=0, dtype=full_type)  115 us
    reduce_scatter x1, waiting for transfers between devices, shards(): lax.psum_scatter(head_term.astype(jnp.bfloat16), 'heads', scatter_dimensi...  101 us
    unnamed x12, waiting for transfers between devices  95.7 us
    dot_general x24, matrix products, scores_of(): jnp.einsum('ijd,ikd->ijk', query_part, key_part, preferred_element_type=j...  92.2 us
  transfers between devices with their start and end apart: 10, of which 8 were waited for; matrix products, arithmetic and copies ran while one was open for 12% of the time, Pallas kernels for 0%

commit v1 on v0

v1 whole, which is shorter than its diff:
```python
import math
import functools
import jax
import jax.numpy as jnp
from jax import lax
from jax.experimental import pallas as pl
from jax.experimental.pallas import tpu as pltpu
from jax.sharding import PartitionSpec as P

EPSILON = 1e-05
LOG2E = 1.4426950408889634
LN2 = 0.6931471805599453
LOW = jnp.bfloat16
FULL = jnp.float32


def dot_nt(a, b):
    return lax.dot_general(a, b, (((1,), (1,)), ((), ())), preferred_element_type=FULL)


def dot_nn(a, b):
    return lax.dot_general(a, b, (((1,), (0,)), ((), ())), preferred_element_type=FULL)


def dot_tn(a, b):
    return lax.dot_general(a, b, (((0,), (0,)), ((), ())), preferred_element_type=FULL)


def normalize(values):
    centre = jnp.mean(values, axis=-1, keepdims=True)
    shifted = values - centre
    spread = lax.rsqrt(jnp.mean(shifted * shifted, axis=-1, keepdims=True) + EPSILON)
    return (shifted * spread, spread)


def main_kernel(
    len_ref, q_ref,
    x_ref, xq_ref, cot_ref, bias_ref,
    wkv_ref, wqg_ref, wo_ref, up_ref, down_ref, gain_ref,
    gkv_in, gqg_in, gout_in, gup_in, gdown_in, ggain_in,
    res_ref, dmid_ref, own0_ref, own1_ref, sib0_ref, sib1_ref, dbias_ref,
    gkv_ref, gqg_ref, gout_ref, gup_ref, gdown_ref, ggain_ref,
    n_s, kv_s, dkv_s, e_s, nq_s, q_s, o_s, r_s, g_s, dos_s, xn_s, hid_s, dpre_s, sh_s, dml_s, gated_s, dqg_s,
    bias_s, dbias_s, dn_s,
    *, start, ib, heads, width, variants, tb, depth, omode, qmode,
):
    item = pl.program_id(0)
    blk = pl.program_id(1)
    length = len_ref[start + item]
    q = q_ref[0]
    res = x_ref.shape[2]
    c = x_ref.shape[3]
    quarter = res // 4
    tokens = ib * quarter
    hj = heads * quarter
    score = 1.0 / math.sqrt(width)

    lane_head = lax.broadcasted_iota(jnp.int32, (1, c), 1) // width
    head_masks = [(lane_head == h).astype(FULL) for h in range(heads)]

    def block_diag(v):
        return jnp.concatenate([(v * m).astype(LOW) for m in head_masks], axis=0)

    diag_mask = (
        lax.broadcasted_iota(jnp.int32, (c, hj), 0) // width
        == lax.broadcasted_iota(jnp.int32, (c, hj), 1) // quarter
    )

    def compact(t):
        t = jnp.where(diag_mask, t, 0.0)
        t = t[:, : hj // 2] + t[:, hj // 2 :]
        t = t.T
        return t[:quarter] + t[quarter:]

    @pl.when(jnp.logical_and(item == 0, blk == 0))
    def _():
        gkv_ref[...] = gkv_in[...]
        gqg_ref[...] = gqg_in[...]
        gout_ref[...] = gout_in[...]
        gup_ref[...] = gup_in[...]
        gdown_ref[...] = gdown_in[...]
        ggain_ref[...] = ggain_in[...]

    @pl.when(blk == 0)
    def _():
        b = bias_ref[0].astype(FULL).T * LOG2E
        real = lax.broadcasted_iota(jnp.int32, (res, hj), 0) < length
        bias_s[...] = jnp.where(real, b, -1e9)
        dbias_s[...] = jnp.zeros_like(dbias_s)

    g0 = gain_ref[0:1, :]
    g1 = gain_ref[1:2, :]
    g2 = gain_ref[2:3, :]
    g3 = gain_ref[3:4, :]

    xq = xq_ref[0].reshape(tokens, c).astype(FULL)
    nq = (normalize(xq)[0] * g0 + g1).astype(LOW)
    nq_s[...] = nq
    qg = dot_nn(nq, wqg_ref[...]).astype(LOW).astype(FULL)
    q_s[...] = (qg[:, :c] * (score * LOG2E)).astype(LOW).reshape(ib, quarter, c)
    g_s[...] = jax.nn.sigmoid(qg[:, c:])

    def pick(t):
        r = t[(heads - 1) * quarter :]
        for h in range(heads - 2, -1, -1):
            r = jnp.where(lane_head == h, t[h * quarter : (h + 1) * quarter], r)
        return r

    def forward(kx):
        x = x_ref[0, :, :kx, :].reshape(ib * kx, c).astype(FULL)
        n = (normalize(x)[0] * g0 + g1).astype(LOW)
        n_s[: ib * kx] = n
        kv_s[: ib * kx] = dot_nn(n, wkv_ref[...]).astype(LOW)
        ones = jnp.ones((kx, c), LOW)

        def scores(i):
            qbd = block_diag(q_s[i].astype(FULL))
            return dot_nt(kv_s[i * kx : (i + 1) * kx, :c], qbd) + bias_s[:kx, :]

        def soft(s):
            return jnp.exp2(s - jnp.max(s, axis=0, keepdims=True)).astype(LOW)

        ahead = [scores(i) for i in range(min(depth, ib))]
        for i in range(ib):
            s = ahead.pop(0)
            if i + depth < ib:
                ahead.append(scores(i + depth))
            eb = soft(s)
            e_s[i * kx : (i + 1) * kx] = eb
            v = kv_s[i * kx : (i + 1) * kx, c:]
            rows = slice(i * quarter, (i + 1) * quarter)
            if omode == 0:
                o = dot_tn(eb, jnp.concatenate([v, ones], axis=1))
                o_s[rows, :] = pick(o[:, :c])
                r_s[rows, :] = 1.0 / pick(o[:, c:])
            else:
                o_s[rows, :] = compact(dot_tn(v, eb))
                total = jnp.sum(eb.astype(FULL), axis=0, keepdims=True)
                r_s[rows, :] = compact(jnp.broadcast_to(1.0 / total, (c, hj)))

    for index, kx in enumerate(variants):
        low = variants[index - 1] if index else 0

        @pl.when(jnp.logical_and(length > low, length <= kx))
        def _():
            forward(kx)

    def middle_part(t, _):
        rows = pl.ds(pl.multiple_of(t * tb, tb), tb)
        per = tb // quarter
        block = pl.ds(t * per, per)
        rinv = r_s[rows, :]
        blended = o_s[rows, :] * rinv
        gate = g_s[rows, :]
        gated = (gate * blended).astype(LOW)
        gated_s[rows, :] = gated
        mid = xq_ref[0, block].reshape(tb, c).astype(FULL) + dot_nn(gated, wo_ref[...])
        n2, spread = normalize(mid)
        shaped = (n2 * g2 + g3).astype(LOW)
        sh_s[rows, :] = shaped
        hp = dot_nn(shaped, up_ref[...])
        sg = 0.5 * jnp.tanh(0.5 * hp) + 0.5
        silu = hp * sg
        hid = silu.astype(LOW)
        hid_s[rows, :] = hid
        res_ref[0, block] = (mid + dot_nn(hid, down_ref[...])).astype(LOW).reshape(per, quarter, c)
        cot = cot_ref[0, block].reshape(tb, c)
        dh = dot_nt(cot, down_ref[...])
        dpre = (dh * (sg + silu * (1.0 - sg))).astype(LOW)
        dpre_s[rows, :] = dpre
        dsh = dot_nt(dpre, up_ref[...])
        ggain_ref[2:3, :] += jnp.sum(dsh * n2, axis=0, keepdims=True)
        ggain_ref[3:4, :] += jnp.sum(dsh, axis=0, keepdims=True)
        u = dsh * g2
        first = jnp.mean(u, axis=-1, keepdims=True)
        second = jnp.mean(u * n2, axis=-1, keepdims=True)
        dmid = cot.astype(FULL) + spread * (u - first - n2 * second)
        dml = dmid.astype(LOW)
        dml_s[rows, :] = dml
        dmid_ref[0, block] = dml.reshape(per, quarter, c)
        dgated = dot_nt(dml, wo_ref[...])
        dblend = dgated * gate
        dqg_s[rows, c:] = (dblend * blended * (1.0 - gate)).astype(LOW)
        dos = (dblend * rinv).astype(LOW)
        dos_s[block] = dos.reshape(per, quarter, c)
        xn_s[block] = (-dos.astype(FULL) * blended).astype(LOW).reshape(per, quarter, c)
        return 0

    lax.fori_loop(0, tokens // tb, middle_part, 0)
    cot_all = cot_ref[0].reshape(tokens, c)
    gdown_ref[...] += dot_tn(cot_all, hid_s[...])
    gup_ref[...] += dot_tn(sh_s[...], dpre_s[...])
    gout_ref[...] += dot_tn(gated_s[...], dml_s[...])

    def backward(kx):
        ones = jnp.ones((kx, c), LOW)

        def d_scores(i):
            dbd = block_diag(dos_s[i].astype(FULL))
            xbd = block_diag(xn_s[i].astype(FULL))
            v_one = jnp.concatenate([kv_s[i * kx : (i + 1) * kx, c:], ones], axis=1)
            return dot_nt(v_one, jnp.concatenate([dbd, xbd], axis=1)), dbd

        ahead = [d_scores(i) for i in range(min(depth, ib))]
        for i in range(ib):
            dp, dbd = ahead.pop(0)
            if i + depth < ib:
                ahead.append(d_scores(i + depth))
            span = slice(i * kx, (i + 1) * kx)
            qbd = block_diag(q_s[i].astype(FULL))
            eb = e_s[span]
            dl = eb.astype(FULL) * dp
            dbias_s[:kx, :] += dl
            dlb = dl.astype(LOW)
            dkv_s[span, c:] = dot_nn(eb, dbd).astype(LOW)
            dkv_s[span, :c] = (dot_nn(dlb, qbd) * LN2).astype(LOW)
            k = kv_s[span, :c]
            if qmode == 0:
                dq = pick(dot_tn(dlb, k))
            else:
                dq = compact(dot_tn(k, dlb))
            dqg_s[i * quarter : (i + 1) * quarter, :c] = (dq * score).astype(LOW)
        dkv = dkv_s[: ib * kx]
        gkv_ref[...] += dot_tn(n_s[: ib * kx], dkv)
        dn_s[:, :kx, :] = dot_nt(dkv, wkv_ref[...]).reshape(ib, kx, c)
        if kx < res:
            dn_s[:, kx:, :] = jnp.zeros((ib, res - kx, c), FULL)

    for index, kx in enumerate(variants):
        low = variants[index - 1] if index else 0

        @pl.when(jnp.logical_and(length > low, length <= kx))
        def _():
            backward(kx)

    own = pl.ds(pl.multiple_of(q * quarter, quarter), quarter)
    dn_s[:, own, :] += dot_nt(dqg_s[...], wqg_ref[...]).reshape(ib, quarter, c)
    y = q // 2
    k = q % 2
    for rel in range(2):
        yy = y if rel == 0 else 1 - y
        keep = pl.ds(pl.multiple_of((yy * 2 + k) * quarter, quarter), quarter)
        send = pl.ds(pl.multiple_of((yy * 2 + 1 - k) * quarter, quarter), quarter)
        (own0_ref, own1_ref)[rel][0] = dn_s[:, keep, :].astype(LOW)
        (sib0_ref, sib1_ref)[rel][0] = dn_s[:, send, :].astype(LOW)
    gqg_ref[...] += dot_tn(nq_s[...], dqg_s[...])

    @pl.when(blk == pl.num_programs(1) - 1)
    def _():
        dbias_ref[0] = dbias_s[...].T.astype(LOW)


def main_call(start, count, lengths, qidx, pair_rep, cot, bias, weights, grads, *, ib=8, variants=(128, 192, 256), tb=512, depth=2, omode=0, qmode=0, interpret=False):
    wkv, wqg, wo, up, down, gains = weights
    items, rl, res, c = pair_rep.shape
    quarter = cot.shape[2]
    hid = up.shape[1]
    heads = 4
    width = c // heads
    ib = min(ib, rl)
    tokens = ib * quarter
    hj = heads * quarter
    grid = (count, rl // ib)

    def whole(shape):
        return pl.BlockSpec(shape, lambda b, i, *_: (0,) * len(shape))

    x_spec = pl.BlockSpec((1, ib, res, c), lambda b, i, ln, q: (start + b, i, 0, 0))
    xq_spec = pl.BlockSpec((1, ib, quarter, c), lambda b, i, ln, q: (start + b, i, q[0], 0))
    cot_spec = pl.BlockSpec((1, ib, quarter, c), lambda b, i, ln, q: (start + b, i, 0, 0))
    out_q = pl.BlockSpec((1, ib, quarter, c), lambda b, i, ln, q: (b, i, 0, 0))
    bias_spec = pl.BlockSpec((1, hj, res), lambda b, i, ln, q: (b, 0, 0))
    grad_shapes = [(c, 2 * c), (c, 2 * c), (c, c), (c, hid), (c, hid), (8, c)]
    kern = functools.partial(
        main_kernel, start=start, ib=ib, heads=heads, width=width, variants=variants, tb=tb, depth=depth, omode=omode, qmode=qmode
    )
    outs = pl.pallas_call(
        kern,
        grid_spec=pltpu.PrefetchScalarGridSpec(
            num_scalar_prefetch=2,
            grid=grid,
            in_specs=[x_spec, xq_spec, cot_spec, bias_spec]
            + [whole(w.shape) for w in (wkv, wqg, wo, up, down, gains)]
            + [whole(s) for s in grad_shapes],
            out_specs=[out_q] * 6 + [bias_spec] + [whole(s) for s in grad_shapes],
            scratch_shapes=[
                pltpu.VMEM((ib * res, c), LOW),
                pltpu.VMEM((ib * res, 2 * c), LOW),
                pltpu.VMEM((ib * res, 2 * c), LOW),
                pltpu.VMEM((ib * res, hj), LOW),
                pltpu.VMEM((tokens, c), LOW),
                pltpu.VMEM((ib, quarter, c), LOW),
                pltpu.VMEM((tokens, c), FULL),
                pltpu.VMEM((tokens, c), FULL),
                pltpu.VMEM((tokens, c), FULL),
                pltpu.VMEM((ib, quarter, c), LOW),
                pltpu.VMEM((ib, quarter, c), LOW),
                pltpu.VMEM((tokens, hid), LOW),
                pltpu.VMEM((tokens, hid), LOW),
                pltpu.VMEM((tokens, c), LOW),
                pltpu.VMEM((tokens, c), LOW),
                pltpu.VMEM((tokens, c), LOW),
                pltpu.VMEM((tokens, 2 * c), LOW),
                pltpu.VMEM((res, hj), FULL),
                pltpu.VMEM((res, hj), FULL),
                pltpu.VMEM((ib, res, c), FULL),
            ],
        ),
        out_shape=[
            jax.ShapeDtypeStruct((count, rl, quarter, c), LOW)
            for _ in range(6)
        ]
        + [jax.ShapeDtypeStruct((count, hj, res), LOW)]
        + [jax.ShapeDtypeStruct(s, FULL) for s in grad_shapes],
        compiler_params=pltpu.CompilerParams(
            dimension_semantics=("arbitrary", "arbitrary"), vmem_limit_bytes=56 * 1024 * 1024
        ),
        interpret=interpret,
        name="layer",
    )(lengths, qidx, pair_rep, pair_rep, cot, bias, wkv, wqg, wo, up, down, gains, *grads)
    return outs


MOMENTUM = 0.9
AVERAGE = 0.6
RATES = (0.5, 0.3, 3.0, 0.05, 0.03, 0.1)
CHUNKS = 4


def update(weight, gradient, moment, average, step_rate, root_pairs):
    moment_next = MOMENTUM * moment + gradient
    weight_next = weight - step_rate / root_pairs * (gradient + MOMENTUM * moment_next)
    return (weight_next, moment_next, AVERAGE * average + (1.0 - AVERAGE) * weight_next)


def norm_back(d_hat, normal, spread):
    first = jnp.mean(d_hat, axis=-1, keepdims=True)
    second = jnp.mean(d_hat * normal, axis=-1, keepdims=True)
    return spread * (d_hat - first - normal * second)


def bias_kernel(q_ref, x_ref, gain_ref, bwt_ref, out_ref):
    _, rl, quarter, c = x_ref.shape
    x = x_ref[0].reshape(rl * quarter, c).astype(FULL)
    n = (normalize(x)[0] * gain_ref[0:1, :] + gain_ref[1:2, :]).astype(LOW)
    out_ref[0] = dot_nt(bwt_ref[...], n).astype(LOW)


def bias_call(qidx, pair_rep, gains, bwt, start, count, quarter):
    items, rl, res, c = pair_rep.shape
    return pl.pallas_call(
        bias_kernel,
        grid_spec=pltpu.PrefetchScalarGridSpec(
            num_scalar_prefetch=1,
            grid=(count,),
            in_specs=[
                pl.BlockSpec((1, rl, quarter, c), lambda b, q: (start + b, 0, q[0], 0)),
                pl.BlockSpec((8, c), lambda b, q: (0, 0)),
                pl.BlockSpec((8, c), lambda b, q: (0, 0)),
            ],
            out_specs=pl.BlockSpec((1, 8, rl * quarter), lambda b, q: (b, 0, 0)),
        ),
        out_shape=jax.ShapeDtypeStruct((count, 8, rl * quarter), LOW),
        compiler_params=pltpu.CompilerParams(vmem_limit_bytes=56 * 1024 * 1024),
        name="bias",
    )(qidx, pair_rep, gains, bwt)


def final_kernel(
    q_ref, x_ref, dmid_ref, own_ref, near_ref, far_ref, dbias_ref, gain_ref, bwt_ref, gin_ref, bin_ref,
    out_ref, ggain_ref, gbias_ref,
):
    _, rl, quarter, c = x_ref.shape
    tokens = rl * quarter

    @pl.when(pl.program_id(0) == 0)
    def _():
        ggain_ref[...] = gin_ref[...]
        gbias_ref[...] = bin_ref[...]

    g0 = gain_ref[0:1, :]
    normal, spread = normalize(x_ref[0].reshape(tokens, c).astype(FULL))
    normed = (normal * g0 + gain_ref[1:2, :]).astype(LOW)
    db = dbias_ref[0]
    gbias_ref[...] += dot_nn(db, normed)
    total = own_ref[0].astype(FULL) + near_ref[0].astype(FULL) + far_ref[0].astype(FULL)
    dn = total.reshape(tokens, c) + dot_tn(db, bwt_ref[...])
    ggain_ref[0:1, :] += jnp.sum(dn * normal, axis=0, keepdims=True)
    ggain_ref[1:2, :] += jnp.sum(dn, axis=0, keepdims=True)
    back = norm_back(dn * g0, normal, spread)
    out_ref[0] = (dmid_ref[0].astype(FULL) + back.reshape(rl, quarter, c)).astype(LOW)


def final_call(qidx, pair_rep, dmid, own, near, far, dbias, gains, bwt, gin, bin_, start, count):
    items, rl, res, c = pair_rep.shape
    quarter = dmid.shape[2]
    one = pl.BlockSpec((1, rl, quarter, c), lambda b, q: (b, 0, 0, 0))
    small = pl.BlockSpec((8, c), lambda b, q: (0, 0))
    return pl.pallas_call(
        final_kernel,
        grid_spec=pltpu.PrefetchScalarGridSpec(
            num_scalar_prefetch=1,
            grid=(count,),
            in_specs=[
                pl.BlockSpec((1, rl, quarter, c), lambda b, q: (start + b, 0, q[0], 0)),
                one, one, one, one,
                pl.BlockSpec((1, 8, rl * quarter), lambda b, q: (b, 0, 0)),
                small, small, small, small,
            ],
            out_specs=[one, small, small],
        ),
        out_shape=[
            jax.ShapeDtypeStruct((count, rl, quarter, c), LOW),
            jax.ShapeDtypeStruct((8, c), FULL),
            jax.ShapeDtypeStruct((8, c), FULL),
        ],
        compiler_params=pltpu.CompilerParams(vmem_limit_bytes=56 * 1024 * 1024),
        name="last",
    )(qidx, pair_rep, dmid, own, near, far, dbias, gains, bwt, gin, bin_)


def shards(
    pair_rep, lengths,
    proj_weight, bias_weight, out_weight, up_weight, down_weight, norm_gains,
    proj_moment, bias_moment, out_moment, up_moment, down_moment, gains_moment,
    proj_average, bias_average, out_average, up_average, down_average, gains_average,
    cotangent,
    *, n_rows, n_heads,
):
    both = ("rows", "heads")
    items, rl, res, c = pair_rep.shape
    quarter = cotangent.shape[2]
    hid = up_weight.shape[1]
    width = out_weight.shape[0]
    n_dev = n_rows * n_heads
    qidx = lax.axis_index("heads").astype(jnp.int32).reshape(1)
    weights = (proj_weight, bias_weight, out_weight, up_weight, down_weight, norm_gains)
    sizes = [w.size for w in weights]
    offs = [sum(sizes[:i]) for i in range(len(sizes))]
    flat = jnp.concatenate([w.astype(LOW).reshape(-1) for w in weights])
    flat = lax.all_gather(flat, both, axis=0, tiled=False)
    part = [flat[:, o : o + s] for o, s in zip(offs, sizes)]
    proj = part[0].reshape(n_rows, n_heads, c // n_rows, 4 * width).transpose(0, 2, 1, 3)
    proj = proj.reshape(c, n_heads, 4, width).transpose(2, 0, 1, 3).reshape(4, c, c)
    wkv = jnp.concatenate([proj[1], proj[2]], axis=1)
    wqg = jnp.concatenate([proj[0], proj[3]], axis=1)
    bwt = part[1].reshape(n_rows, n_heads, c // n_rows).transpose(1, 0, 2).reshape(n_heads, c)
    bwt = jnp.pad(bwt, ((0, 8 - n_heads), (0, 0)))
    wo = part[2].reshape(n_rows, n_heads, width, c // n_rows).transpose(1, 2, 0, 3).reshape(c, c)
    up = part[3].reshape(c, hid)
    down = part[4].reshape(hid, c)
    gains = part[5].reshape(n_dev, 4, c // n_dev).transpose(1, 0, 2).reshape(4, c).astype(FULL)
    gains = jnp.pad(gains, ((0, 4), (0, 0)))
    kern_weights = (wkv, wqg, wo, up, down, gains)

    group = n_rows // n_heads
    to_bias = [
        (r * n_heads + q, ((r % group) * n_heads + q) * n_heads + r // group)
        for r in range(n_rows) for q in range(n_heads)
    ]
    from_bias = [(b, a) for a, b in to_bias]
    core = [(d, d ^ 1) for d in range(n_dev)]
    cross = [(d, d ^ 2) for d in range(n_dev)]
    count = items // CHUNKS

    biases = []
    for ch in range(CHUNKS):
        piece = bias_call(qidx, pair_rep, gains, bwt, ch * count, count, quarter)
        piece = piece[:, :n_heads].reshape(count, n_heads, rl, quarter)
        piece = lax.ppermute(piece, both, to_bias)
        allb = lax.all_gather(piece, "rows", axis=0, tiled=False)
        allb = allb.reshape(group, n_heads, count, n_heads, rl, quarter).transpose(2, 3, 0, 4, 1, 5)
        biases.append(allb.reshape(count, n_heads * quarter, res))

    grads = [jnp.zeros(s, FULL) for s in [(c, 2 * c), (c, 2 * c), (c, c), (c, hid), (c, hid), (8, c)]]
    results = []
    pairs = []
    ggain = jnp.zeros((8, c), FULL)
    gbias = jnp.zeros((8, c), FULL)
    for ch in range(CHUNKS):
        outs = main_call(ch * count, count, lengths, qidx, pair_rep, cotangent, biases[ch], kern_weights, grads)
        res_c, dmid, own0, own1, sib0, sib1, dbias = outs[:7]
        grads = list(outs[7:])
        results.append(res_c)
        near1 = lax.ppermute(sib1, both, core)
        near0 = lax.ppermute(sib0, both, core)
        far = lax.ppermute((own1.astype(FULL) + near1.astype(FULL)).astype(LOW), both, cross)
        dbias = dbias.reshape(count, n_heads, group, rl, n_heads, quarter).transpose(2, 4, 0, 1, 3, 5)
        dbias = dbias.reshape(n_rows, count, n_heads, rl, quarter)
        dbias = lax.psum_scatter(dbias, "rows", scatter_dimension=0, tiled=False)
        dbias = lax.ppermute(dbias, both, from_bias)
        dbias = jnp.pad(dbias.reshape(count, n_heads, rl * quarter), ((0, 0), (0, 8 - n_heads), (0, 0)))
        dp, ggain, gbias = final_call(
            qidx, pair_rep, dmid, own0, near0, far, dbias, gains, bwt, ggain, gbias, ch * count, count
        )
        pairs.append(dp)

    gkv, gqg, gout, gup, gdown, gtwo = grads
    gproj = jnp.stack([gqg[:, :c], gkv[:, :c], gkv[:, c:], gqg[:, c:]]).reshape(4, c, n_heads, width)
    gproj = gproj.transpose(1, 2, 0, 3).reshape(n_rows, c // n_rows, n_heads, 4 * width).transpose(0, 2, 1, 3)
    gb = gbias[:n_heads].reshape(n_heads, n_rows, c // n_rows).transpose(1, 0, 2)
    go = gout.reshape(n_heads, width, n_rows, c // n_rows).transpose(2, 0, 1, 3)
    gg = jnp.concatenate([ggain[:2], gtwo[2:4]]).reshape(4, n_dev, c // n_dev).transpose(1, 0, 2)
    flat = jnp.concatenate(
        [g.reshape(n_dev, -1) for g in (gproj, gb, go, gup, gdown.T, gg)], axis=1
    )
    flat = lax.psum_scatter(flat, both, scatter_dimension=0, tiled=False)
    sums = [flat[o : o + s].reshape(w.shape) for o, s, w in zip(offs, sizes, weights)]
    moments = (proj_moment, bias_moment, out_moment, up_moment, down_moment, gains_moment)
    averages = (proj_average, bias_average, out_average, up_average, down_average, gains_average)
    root_pairs = math.sqrt(items * res * res)
    nexts = [
        update(w, g, m, a, rate, root_pairs)
        for w, g, m, a, rate in zip(weights, sums, moments, averages, RATES)
    ]
    return (
        jnp.concatenate(results, axis=0),
        jnp.concatenate(pairs, axis=0),
        *[n[0] for n in nexts],
        *[n[1] for n in nexts],
        *[n[2] for n in nexts],
    )


def solution(mesh):
    weight_specs = (
        P("rows", "heads"),
        P("rows", "heads"),
        P("heads", "rows"),
        P(("rows", "heads"), None),
        P(("rows", "heads"), None),
        P(None, ("rows", "heads")),
    )
    quarter_spec = P(None, "rows", "heads", None)
    in_specs = (P(None, "rows", None, None), P()) + weight_specs * 3 + (quarter_spec,)
    out_specs = (quarter_spec, quarter_spec) + weight_specs * 3
    body = functools.partial(shards, n_rows=mesh.shape["rows"], n_heads=mesh.shape["heads"])
    return jax.shard_map(body, mesh=mesh, in_specs=in_specs, out_specs=out_specs, check_vma=False)
```

time: 2240 us -> 1070 us (0.48)
  matrix products: 639 us -> 0 us
  other arithmetic: 391 us -> 35.9 us
  Pallas kernels: 0 us -> 355 us
  waiting for transfers between devices: 772 us -> 424 us
  local copies, waits for them, and re-layouts: 169 us -> 58.4 us
  blocking collectives: 236 us -> 153 us
    dot_general x98 -> x0, matrix products: 639 us -> none  [the longest x5 124 us: flat_product(): jnp.einsum('na,nb->ab', left.reshape(-1, left.shape[-1]), right.reshape(-...]
    reduce_scatter x6 -> x4, waiting for transfers between devices: 524 us -> 115 us  [shards(): dbias = lax.psum_scatter(dbias, 'rows', scatter_dimension=0, tiled=False)]
    pallas_call x0 -> x12, Pallas kernels: none -> 355 us  [the longest x4 306 us: main_call(): pl.pallas_call(kern, grid_spec=pltpu.PrefetchScalarGridSpec(num_scalar_pr...]
    reduce_sum x30 -> x0, other arithmetic: 233 us -> none  [the longest x12 115 us: attend_back(): d_bias_item = jnp.sum(d_logits, axis=0, dtype=full_type)]
    unnamed x12 -> x8, waiting for transfers between devices: 95.7 us -> 253 us
    all_gather x2 -> x0, waiting for transfers between devices: 152 us -> none  [the longest x1 152 us: shards(): d_rows = lax.all_gather(d_middle_low, 'heads', axis=2, tiled=True)]
    while x26 -> x0, local copies, waits for them, and re-layouts: 74 us -> none
    convert_element_type x7 -> x6, other arithmetic: 81.7 us -> 15.6 us  [the longest x4 14.2 us: shards(): (own1.astype(FULL) + near1.astype(FULL)).astype(LOW)]
  transfers between devices with their start and end apart: 10 -> 26, of which waited for: 8 -> 7; matrix products, arithmetic and copies ran while one was open for 12% -> 6% of each run, Pallas kernels for 0% -> 25%
where the time goes in v1:
time: 1070 us; the launch traced here: 1060 us
  waiting for transfers between devices  424 us (40%)
  Pallas kernels  355 us (33%)
  blocking collectives  153 us (14%)
  local copies, waits for them, and re-layouts  58.4 us (5%)
  other arithmetic  35.9 us (3%)
  starting transfers between devices  18.4 us (2%)
  between operations  15.1 us (1%)
    pallas_call x4, Pallas kernels, main_call(): pl.pallas_call(kern, grid_spec=pltpu.PrefetchScalarGridSpec(num_scalar_pr...  306 us
    unnamed x8, waiting for transfers between devices  253 us
    all_gather x4, blocking collectives, shards(): allb = lax.all_gather(piece, 'rows', axis=0, tiled=False)  153 us
    reduce_scatter x4, waiting for transfers between devices, shards(): dbias = lax.psum_scatter(dbias, 'rows', scatter_dimension=0, tiled=False)  115 us
    ppermute x4, waiting for transfers between devices, shards(): lax.ppermute((own1.astype(FULL) + near1.astype(FULL)).astype(LOW), both,...  54.7 us
    pallas_call x4, Pallas kernels, final_call(): pl.pallas_call(final_kernel, grid_spec=pltpu.PrefetchScalarGridSpec(num_s...  31.6 us
  transfers between devices with their start and end apart: 26, of which 7 were waited for; matrix products, arithmetic and copies ran while one was open for 6% of the time, Pallas kernels for 25%

profile of v1, /device:TPU:0, one launch (start us, length us, event | category | flops | bytes accessed | tf_op | source)
XLA Modules:
  0.0 1059.3 jit_solution(16268849799527086797)
XLA Ops:
  12.4 130.1 %all-reduce.11.cloned.1.call-done = bf16[214016]{0:T(1024)(128)(2,1)} async-done(((bf16[214016]{0:T(1024)(128)(2,1)}), bf16[214016]{0:T(1024)(128)(2,1)}) %all-reduce.11.cloned.1.call-update) | async-done | bytes 428048
  145.9 4.3 bias.4
  158.2 36.8 %all-gather.1 = bf16[24,4,32,64]{3,2,1,0:T(8,128)(2,1)S(1)} all-gather(bf16[3,4,32,64]{3,2,1,0:T(8,128)(2,1)S(1)} %collective-permute-done), channel_id=3, replica_groups=mesh['rows'=8,'heads'=4] {'rows'}, dimensions={0}, use_global_device_ids=true | all-gather | bytes 442368 | tf_op jit(solution)/shard_map/all_gather | solution.py:471
  199.5 81.3 %layer.4 = (bf16[3,32,64,128]{3,2,1,0:T(8,128)(2,1)}, bf16[3,32,64,128]{3,2,1,0:T(8,128)(2,1)}, bf16[3,32,64,128]{3,2,1,0:T(8,128)(2,1)}, bf16[3,32,64,128]{3,2,...) custom-call(s32[12]{0:T(128)} %len_ref.7, ...), custom_call_target="tpu_custom_call" | custom-call | tf_op jit(solution)/shard_map/layer/pallas_call | solution.py:277
  283.8 4.7 bias.5
  290.2 39.7 %all-gather.2 = bf16[24,4,32,64]{3,2,1,0:T(8,128)(2,1)S(1)} all-gather(bf16[3,4,32,64]{3,2,1,0:T(8,128)(2,1)S(1)} %collective-permute-done.1), channel_id=4, replica_groups=mesh['rows'=8,'heads'=4] {'rows'}, dimensions={0}, use_global_device_ids=true | all-gather | bytes 442368 | tf_op jit(solution)/shard_map/all_gather | solution.py:471
  331.8 76.4 %layer.5 = (bf16[3,32,64,128]{3,2,1,0:T(8,128)(2,1)}, bf16[3,32,64,128]{3,2,1,0:T(8,128)(2,1)}, bf16[3,32,64,128]{3,2,1,0:T(8,128)(2,1)}, bf16[3,32,64,128]{3,2,...) custom-call(s32[12]{0:T(128)} %len_ref.7, ...), custom_call_target="tpu_custom_call" | custom-call | tf_op jit(solution)/shard_map/layer/pallas_call | solution.py:277
  411.9 4.3 bias.6
  417.9 41.4 %all-gather.3 = bf16[24,4,32,64]{3,2,1,0:T(8,128)(2,1)S(1)} all-gather(bf16[3,4,32,64]{3,2,1,0:T(8,128)(2,1)S(1)} %collective-permute-done.2), channel_id=5, replica_groups=mesh['rows'=8,'heads'=4] {'rows'}, dimensions={0}, use_global_device_ids=true | all-gather | bytes 442368 | tf_op jit(solution)/shard_map/all_gather | solution.py:471
  461.1 75.8 %layer.6 = (bf16[3,32,64,128]{3,2,1,0:T(8,128)(2,1)}, bf16[3,32,64,128]{3,2,1,0:T(8,128)(2,1)}, bf16[3,32,64,128]{3,2,1,0:T(8,128)(2,1)}, bf16[3,32,64,128]{3,2,...) custom-call(s32[12]{0:T(128)} %len_ref.7, ...), custom_call_target="tpu_custom_call" | custom-call | tf_op jit(solution)/shard_map/layer/pallas_call | solution.py:277
  540.0 4.7 bias.7
  549.5 59.2 %reduce-scatter.9.cloned.1.call-done = bf16[1,3,4,32,64]{4,3,2,1,0:T(8,128)(2,1)} async-done(((bf16[8,3,4,32,64]{4,3,2,1,0:T(8,128)(2,1)}), bf16[1,3,4,32,64]{4,3,2,1,0:T(8,128)(2,1)}) %reduce-scatter.9.cloned.1.call-update) | async-done | bytes 49168 | tf_op jit(solution)/shard_map/reduce_scatter | solution.py:490
  610.2 34.8 %all-gather.4 = bf16[24,4,32,64]{3,2,1,0:T(8,128)(2,1)S(1)} all-gather(bf16[3,4,32,64]{3,2,1,0:T(8,128)(2,1)S(1)} %collective-permute-done.3), channel_id=6, replica_groups=mesh['rows'=8,'heads'=4] {'rows'}, dimensions={0}, use_global_device_ids=true | all-gather | bytes 442368 | tf_op jit(solution)/shard_map/all_gather | solution.py:471
  646.9 72.4 %layer.7 = (bf16[3,32,64,128]{3,2,1,0:T(8,128)(2,1)}, bf16[3,32,64,128]{3,2,1,0:T(8,128)(2,1)}, bf16[3,32,64,128]{3,2,1,0:T(8,128)(2,1)}, bf16[3,32,64,128]{3,2,...) custom-call(s32[12]{0:T(128)} %len_ref.7, ...), custom_call_target="tpu_custom_call" | custom-call | tf_op jit(solution)/shard_map/layer/pallas_call | solution.py:277
  720.6 3.4 add_convert_fusion.3
  726.6 4.0 add_convert_fusion.2
  730.6 56.2 %reduce-scatter.11.cloned.1.call-done = bf16[1,3,4,32,64]{4,3,2,1,0:T(8,128)(2,1)} async-done(((bf16[8,3,4,32,64]{4,3,2,1,0:T(8,128)(2,1)}), bf16[1,3,4,32,64]{4,3,2,1,0:T(8,128)(2,1)}) %reduce-scatter.11.cloned.1.call-update) | async-done | bytes 49168 | tf_op jit(solution)/shard_map/reduce_scatter | solution.py:490
  788.4 3.4 add_convert_fusion.1
  793.7 3.0 collective-permute-start.10
  796.8 3.4 add_convert_fusion
  800.4 1.9 collective-permute-start.18
  811.1 5.8 pad_maximum_fusion
  821.0 8.2 last.4
  829.1 3.1 collective-permute-done.10.far_ref
  832.2 7.7 last.5
  840.0 26.0 %collective-permute-done.14.far_ref = bf16[3,32,64,128]{3,2,1,0:T(8,128)(2,1)} collective-permute-done((bf16[3,32,64,128]{3,2,1,0:T(8,128)(2,1)}, bf16[3,32,64,128]{3,2,1,0:T(8,128)(2,1)}, u32[]{:S(2)}, u32[]{:S(2)}) %collective-permute-start.14) | collective-permute-done | bytes 1572896 | tf_op jit(solution)/shard_map/ppermute | solution.py:487
  865.9 7.7 last.6
  873.7 25.7 %collective-permute-done.18.far_ref = bf16[3,32,64,128]{3,2,1,0:T(8,128)(2,1)} collective-permute-done((bf16[3,32,64,128]{3,2,1,0:T(8,128)(2,1)}, bf16[3,32,64,128]{3,2,1,0:T(8,128)(2,1)}, u32[]{:S(2)}, u32[]{:S(2)}) %collective-permute-start.18) | collective-permute-done | bytes 1572896 | tf_op jit(solution)/shard_map/ppermute | solution.py:487
  899.4 7.9 last.7
  911.7 2.2 concatenate.28
  914.2 6.2 pad_maximum_fusion.1
  920.3 123.3 %all-reduce.13.cloned.1.call-done = f32[32,6688]{1,0:T(8,128)} async-done(((f32[32,6688]{1,0:T(8,128)}), f32[32,6688]{1,0:T(8,128)}) %all-reduce.13.cloned.1.call-update) | async-done | bytes 856080
  (257 shorter events, 79.5 us)
Async XLA Ops:
  7.2 135.2 %all-reduce.11.cloned.1.call-start = ((), (), s32[]{:S(2)}) async-start(), calls=%async_computation.8 | async-start | bytes 856064
  12.3 534.1 %reduce-scatter.5.cloned.1.call-start = ((), (), s32[]{:S(2)}) async-start(), calls=%async_computation.4 | async-start | bytes 884736 | tf_op jit(solution)/shard_map/reduce_scatter | solution.py:490
  151.2 7.0 collective-permute-start
  283.7 264.2 %reduce-scatter.7.cloned.1.call-start = ((), (), s32[]{:S(2)}) async-start(), calls=%async_computation.5 | async-start | bytes 884736 | tf_op jit(solution)/shard_map/reduce_scatter | solution.py:490
  289.5 0.7 collective-permute-start.1
  411.1 197.6 %reduce-scatter.9.cloned.1.call-start = ((), (), s32[]{:S(2)}) async-start(), calls=%async_computation.6 | async-start | bytes 884736 | tf_op jit(solution)/shard_map/reduce_scatter | solution.py:490
  411.3 309.1 %collective-permute-start.5 = (bf16[3,32,64,128]{3,2,1,0:T(8,128)(2,1)}, bf16[3,32,64,128]{3,2,1,0:T(8,128)(2,1)}, u32[]{:S(2)}, u32[]{:S(2)}) collective-permute-start(bf16[3,32,64,128]{3,2,1,0:T(8,128)(2,1)} %get-tuple-element.110), channel_id=1, source_target_pairs={{0,1},{1,0},{2,3},{3,2},{4,5},{5,4},{6,7},{7,6},{8,9},{9,8},{10,11... | collective-permute-start | bytes 4718600 | tf_op jit(solution)/shard_map/ppermute | solution.py:485
  411.4 312.6 %collective-permute-start.9 = (bf16[3,32,64,128]{3,2,1,0:T(8,128)(2,1)}, bf16[3,32,64,128]{3,2,1,0:T(8,128)(2,1)S(1)}, u32[]{:S(2)}, u32[]{:S(2)}) collective-permute-start(bf16[3,32,64,128]{3,2,1,0:T(8,128)(2,1)} %get-tuple-element.117), channel_id=1, source_target_pairs={{0,1},{1,0},{2,3},{3,2},{4,5},{5,4},{6,7},{7,6},{8,9},{9,8},{10,11... | collective-permute-start | bytes 4718600 | tf_op jit(solution)/shard_map/ppermute | solution.py:485
  417.2 0.7 collective-permute-start.2
  539.8 247.0 %reduce-scatter.11.cloned.1.call-start = ((), (), s32[]{:S(2)}) async-start(), calls=%async_computation.7 | async-start | bytes 884736 | tf_op jit(solution)/shard_map/reduce_scatter | solution.py:490
  539.9 246.9 %collective-permute-start.13 = (bf16[3,32,64,128]{3,2,1,0:T(8,128)(2,1)}, bf16[3,32,64,128]{3,2,1,0:T(8,128)(2,1)}, u32[]{:S(2)}, u32[]{:S(2)}) collective-permute-start(bf16[3,32,64,128]{3,2,1,0:T(8,128)(2,1)} %get-tuple-element.126), channel_id=1, source_target_pairs={{0,1},{1,0},{2,3},{3,2},{4,5},{5,4},{6,7},{7,6},{8,9},{9,8},{10,11... | collective-permute-start | bytes 4718600 | tf_op jit(solution)/shard_map/ppermute | solution.py:485
  545.7 2.3 collective-permute-start.3
  546.4 62.3 %collective-permute-start.7 = (bf16[3,4,32,64]{3,2,1,0:T(8,128)(2,1)}, bf16[3,4,32,64]{3,2,1,0:T(8,128)(2,1)S(1)}, u32[]{:S(2)}, u32[]{:S(2)}) collective-permute-start(bf16[3,4,32,64]{3,2,1,0:T(8,128)(2,1)} %bitcast.137), channel_id=1, source_target_pairs={{0,0},{4,1},{8,2},{12,3},{16,4},{20,5},{24,6},{28,7},{1,8},{5,9},{... | collective-permute-start | bytes 147464 | tf_op jit(solution)/shard_map/ppermute | solution.py:491
  548.0 171.3 %collective-permute-start.11 = (bf16[3,4,32,64]{3,2,1,0:T(8,128)(2,1)}, bf16[3,4,32,64]{3,2,1,0:T(8,128)(2,1)S(1)}, u32[]{:S(2)}, u32[]{:S(2)}) collective-permute-start(bf16[3,4,32,64]{3,2,1,0:T(8,128)(2,1)} %bitcast.138), channel_id=1, source_target_pairs={{0,0},{4,1},{8,2},{12,3},{16,4},{20,5},{24,6},{28,7},{1,8},{5,9},{... | collective-permute-start | bytes 147464 | tf_op jit(solution)/shard_map/ppermute | solution.py:491
  608.7 111.3 %collective-permute-start.15 = (bf16[3,4,32,64]{3,2,1,0:T(8,128)(2,1)}, bf16[3,4,32,64]{3,2,1,0:T(8,128)(2,1)S(1)}, u32[]{:S(2)}, u32[]{:S(2)}) collective-permute-start(bf16[3,4,32,64]{3,2,1,0:T(8,128)(2,1)} %bitcast.139), channel_id=1, source_target_pairs={{0,0},{4,1},{8,2},{12,3},{16,4},{20,5},{24,6},{28,7},{1,8},{5,9},{... | collective-permute-start | bytes 147464 | tf_op jit(solution)/shard_map/ppermute | solution.py:491
  719.9 73.7 %collective-permute-start.4 = (bf16[3,32,64,128]{3,2,1,0:T(8,128)(2,1)}, bf16[3,32,64,128]{3,2,1,0:T(8,128)(2,1)S(1)}, u32[]{:S(2)}, u32[]{:S(2)}) collective-permute-start(bf16[3,32,64,128]{3,2,1,0:T(8,128)(2,1)} %get-tuple-element.108), channel_id=1, source_target_pairs={{0,1},{1,0},{2,3},{3,2},{4,5},{5,4},{6,7},{7,6},{8,9},{9,8},{10,11... | collective-permute-start | bytes 4718600 | tf_op jit(solution)/shard_map/ppermute | solution.py:486
  720.0 76.7 %collective-permute-start.17 = (bf16[3,32,64,128]{3,2,1,0:T(8,128)(2,1)}, bf16[3,32,64,128]{3,2,1,0:T(8,128)(2,1)}, u32[]{:S(2)}, u32[]{:S(2)}) collective-permute-start(bf16[3,32,64,128]{3,2,1,0:T(8,128)(2,1)} %get-tuple-element.135), channel_id=1, source_target_pairs={{0,1},{1,0},{2,3},{3,2},{4,5},{5,4},{6,7},{7,6},{8,9},{9,8},{10,11... | collective-permute-start | bytes 4718600 | tf_op jit(solution)/shard_map/ppermute | solution.py:485
  720.5 79.7 %collective-permute-start.8 = (bf16[3,32,64,128]{3,2,1,0:T(8,128)(2,1)}, bf16[3,32,64,128]{3,2,1,0:T(8,128)(2,1)}, u32[]{:S(2)}, u32[]{:S(2)}) collective-permute-start(bf16[3,32,64,128]{3,2,1,0:T(8,128)(2,1)} %get-tuple-element.115), channel_id=1, source_target_pairs={{0,1},{1,0},{2,3},{3,2},{4,5},{5,4},{6,7},{7,6},{8,9},{9,8},{10,11... | collective-permute-start | bytes 4718600 | tf_op jit(solution)/shard_map/ppermute | solution.py:486
  724.0 76.4 %collective-permute-start.6 = (bf16[3,32,64,128]{3,2,1,0:T(8,128)(2,1)}, bf16[3,32,64,128]{3,2,1,0:T(8,128)(2,1)}, u32[]{:S(2)}, u32[]{:S(2)}) collective-permute-start(bf16[3,32,64,128]{3,2,1,0:T(8,128)(2,1)} %add_convert_fusion.3), channel_id=1, source_target_pairs={{0,2},{1,3},{2,0},{3,1},{4,6},{5,7},{6,4},{7,5},{8,10},{9,11},{10,... | collective-permute-start | bytes 4718600 | tf_op jit(solution)/shard_map/ppermute | solution.py:487
  726.5 317.1 %all-reduce.13.cloned.1.call-start = ((), (), s32[]{:S(2)}) async-start(), calls=%async_computation.9 | async-start | bytes 1736704
  786.8 5.0 collective-permute-start.19
  791.8 48.1 %collective-permute-start.12 = (bf16[3,32,64,128]{3,2,1,0:T(8,128)(2,1)}, bf16[3,32,64,128]{3,2,1,0:T(8,128)(2,1)}, u32[]{:S(2)}, u32[]{:S(2)}) collective-permute-start(bf16[3,32,64,128]{3,2,1,0:T(8,128)(2,1)} %get-tuple-element.124), channel_id=1, source_target_pairs={{0,1},{1,0},{2,3},{3,2},{4,5},{5,4},{6,7},{7,6},{8,9},{9,8},{10,11... | collective-permute-start | bytes 4718600 | tf_op jit(solution)/shard_map/ppermute | solution.py:486
  793.7 38.6 %collective-permute-start.10 = (bf16[3,32,64,128]{3,2,1,0:T(8,128)(2,1)}, bf16[3,32,64,128]{3,2,1,0:T(8,128)(2,1)}, u32[]{:S(2)}, u32[]{:S(2)}) collective-permute-start(bf16[3,32,64,128]{3,2,1,0:T(8,128)(2,1)} %add_convert_fusion.2), channel_id=1, source_target_pairs={{0,2},{1,3},{2,0},{3,1},{4,6},{5,7},{6,4},{7,5},{8,10},{9,11},{10,... | collective-permute-start | bytes 4718600 | tf_op jit(solution)/shard_map/ppermute | solution.py:487
  796.6 69.3 %collective-permute-start.14 = (bf16[3,32,64,128]{3,2,1,0:T(8,128)(2,1)}, bf16[3,32,64,128]{3,2,1,0:T(8,128)(2,1)}, u32[]{:S(2)}, u32[]{:S(2)}) collective-permute-start(bf16[3,32,64,128]{3,2,1,0:T(8,128)(2,1)} %add_convert_fusion.1), channel_id=1, source_target_pairs={{0,2},{1,3},{2,0},{3,1},{4,6},{5,7},{6,4},{7,5},{8,10},{9,11},{10,... | collective-permute-start | bytes 4718600 | tf_op jit(solution)/shard_map/ppermute | solution.py:487
  800.2 73.5 %collective-permute-start.16 = (bf16[3,32,64,128]{3,2,1,0:T(8,128)(2,1)}, bf16[3,32,64,128]{3,2,1,0:T(8,128)(2,1)S(1)}, u32[]{:S(2)}, u32[]{:S(2)}) collective-permute-start(bf16[3,32,64,128]{3,2,1,0:T(8,128)(2,1)} %get-tuple-element.133), channel_id=1, source_target_pairs={{0,1},{1,0},{2,3},{3,2},{4,5},{5,4},{6,7},{7,6},{8,9},{9,8},{10,11... | collective-permute-start | bytes 4718600 | tf_op jit(solution)/shard_map/ppermute | solution.py:486
  800.4 99.0 %collective-permute-start.18 = (bf16[3,32,64,128]{3,2,1,0:T(8,128)(2,1)}, bf16[3,32,64,128]{3,2,1,0:T(8,128)(2,1)}, u32[]{:S(2)}, u32[]{:S(2)}) collective-permute-start(bf16[3,32,64,128]{3,2,1,0:T(8,128)(2,1)} %add_convert_fusion), channel_id=1, source_target_pairs={{0,2},{1,3},{2,0},{3,1},{4,6},{5,7},{6,4},{7,5},{8,10},{9,11},{10,... | collective-permute-start | bytes 4718600 | tf_op jit(solution)/shard_map/ppermute | solution.py:487
  914.1 136.3 %copy-start.36 = (f32[4,4]{1,0:T(4,128)S(1)}, f32[4,4]{1,0:T(4,128)}, u32[]{:S(2)}) copy-start(f32[4,4]{1,0:T(4,128)} %param.28) | copy-start | bytes 196
  914.1 136.3 %copy-start.37 = (f32[4,4]{1,0:T(4,128)S(1)}, f32[4,4]{1,0:T(4,128)}, u32[]{:S(2)}) copy-start(f32[4,4]{1,0:T(4,128)} %param.40) | copy-start | bytes 196
  914.1 136.3 %copy-start.38 = (f32[4,4]{1,0:T(4,128)S(1)}, f32[4,4]{1,0:T(4,128)}, u32[]{:S(2)}) copy-start(f32[4,4]{1,0:T(4,128)} %param.34) | copy-start | bytes 196
  914.1 136.9 %copy-start.39 = (f32[16,1]{0,1:T(1,128)S(1)}, f32[16,1]{0,1:T(1,128)}, u32[]{:S(2)}) copy-start(f32[16,1]{0,1:T(1,128)} %param.24) | copy-start | bytes 196
  914.1 136.8 %copy-start.40 = (f32[16,1]{0,1:T(1,128)S(1)}, f32[16,1]{0,1:T(1,128)}, u32[]{:S(2)}) copy-start(f32[16,1]{0,1:T(1,128)} %param.36) | copy-start | bytes 196
  914.1 136.8 %copy-start.41 = (f32[16,1]{0,1:T(1,128)S(1)}, f32[16,1]{0,1:T(1,128)}, u32[]{:S(2)}) copy-start(f32[16,1]{0,1:T(1,128)} %param.30) | copy-start | bytes 196
  (36 other events, 1797.3 us)
Sparse Core Ops, SparseCore 0:
  13.9 128.4 all-reduce.10
  283.9 63.2 reduce-scatter.4
  411.2 66.8 reduce-scatter.6
  540.0 68.6 reduce-scatter.8
  726.7 60.1 reduce-scatter.10
  914.1 129.5 all-reduce.12

commit v2 on v1

v2 whole, which is shorter than its diff:
```python
import math
import functools
import jax
import jax.numpy as jnp
from jax import lax
from jax.experimental import pallas as pl
from jax.experimental.pallas import tpu as pltpu
from jax.sharding import PartitionSpec as P

EPSILON = 1e-05
LOG2E = 1.4426950408889634
LN2 = 0.6931471805599453
LOW = jnp.bfloat16
FULL = jnp.float32


def dot_nt(a, b):
    return lax.dot_general(a, b, (((1,), (1,)), ((), ())), preferred_element_type=FULL)


def dot_nn(a, b):
    return lax.dot_general(a, b, (((1,), (0,)), ((), ())), preferred_element_type=FULL)


def dot_tn(a, b):
    return lax.dot_general(a, b, (((0,), (0,)), ((), ())), preferred_element_type=FULL)


def normalize(values):
    centre = jnp.mean(values, axis=-1, keepdims=True)
    shifted = values - centre
    spread = lax.rsqrt(jnp.mean(shifted * shifted, axis=-1, keepdims=True) + EPSILON)
    return (shifted * spread, spread)


def main_kernel(
    len_ref, q_ref,
    x_ref, xq_ref, cot_ref, bias_ref,
    wkv_ref, wqg_ref, wo_ref, up_ref, down_ref, gain_ref,
    gkv_in, gqg_in, gout_in, gup_in, gdown_in, ggain_in,
    *rest,
    start, ib, heads, width, variants, tb, depth, rl,
):
    (
        res_ref, dmid_ref, own0_ref, own1_ref, sib0_ref, sib1_ref, dbias_ref,
        gkv_ref, gqg_ref, gout_ref, gup_ref, gdown_ref, ggain_ref,
        n_s, kv_s, dkv_s, e_s, nq_s, q_s, o_s, r_s, g_s, dos_s, xn_s, hid_s, dpre_s, sh_s, dml_s, gated_s, dqg_s,
        bias_s, dbias_s, dn_s,
    ) = rest[-33:]
    item = pl.program_id(0)
    blk = pl.program_id(1)
    length = len_ref[start + item]
    q = q_ref[0]
    res = x_ref.shape[2]
    c = x_ref.shape[3]
    quarter = res // 4
    tokens = ib * quarter
    hj = heads * quarter
    score = 1.0 / math.sqrt(width)

    lane_head = lax.broadcasted_iota(jnp.int32, (1, c), 1) // width
    head_masks = [(lane_head == h).astype(FULL) for h in range(heads)]

    def block_diag(v):
        v = v.astype(FULL)
        parts = [v[g * rl : (g + 1) * rl] * m for g in range(quarter // rl) for m in head_masks]
        if rl % 16 == 0:
            return jnp.concatenate([p.astype(LOW) for p in parts], axis=0)
        return jnp.concatenate(parts, axis=0).astype(LOW)

    def pick(t):
        parts = []
        for g in range(quarter // rl):
            base = g * heads * rl
            r = t[base + (heads - 1) * rl : base + heads * rl]
            for h in range(heads - 2, -1, -1):
                r = jnp.where(lane_head == h, t[base + h * rl : base + (h + 1) * rl], r)
            parts.append(r)
        return jnp.concatenate(parts, axis=0)

    @pl.when(jnp.logical_and(item == 0, blk == 0))
    def _():
        gkv_ref[...] = gkv_in[...]
        gqg_ref[...] = gqg_in[...]
        gout_ref[...] = gout_in[...]
        gup_ref[...] = gup_in[...]
        gdown_ref[...] = gdown_in[...]
        ggain_ref[...] = ggain_in[...]

    @pl.when(blk == 0)
    def _():
        b = jnp.concatenate([bias_ref[0, g] for g in range(quarter // rl)], axis=1).astype(FULL) * LOG2E
        real = lax.broadcasted_iota(jnp.int32, (res, hj), 0) < length
        bias_s[...] = jnp.where(real, b, -1e9)
        dbias_s[...] = jnp.zeros_like(dbias_s)

    g0 = gain_ref[0:1, :]
    g1 = gain_ref[1:2, :]
    g2 = gain_ref[2:3, :]
    g3 = gain_ref[3:4, :]

    xq = xq_ref[0].reshape(tokens, c).astype(FULL)
    nq = (normalize(xq)[0] * g0 + g1).astype(LOW)
    nq_s[...] = nq
    qg = dot_nn(nq, wqg_ref[...]).astype(LOW).astype(FULL)
    q_s[...] = (qg[:, :c] * (score * LOG2E)).astype(LOW).reshape(ib, quarter, c)
    g_s[...] = jax.nn.sigmoid(qg[:, c:])

    def forward(kx):
        x = x_ref[0, :, :kx, :].reshape(ib * kx, c).astype(FULL)
        n = (normalize(x)[0] * g0 + g1).astype(LOW)
        n_s[: ib * kx] = n
        kv_s[: ib * kx] = dot_nn(n, wkv_ref[...]).astype(LOW)
        ones = jnp.ones((kx, c), LOW)

        def scores(i):
            qbd = block_diag(q_s[i])
            return dot_nt(kv_s[i * kx : (i + 1) * kx, :c], qbd) + bias_s[:kx, :]

        def soft(s):
            return jnp.exp2(s - jnp.max(s, axis=0, keepdims=True)).astype(LOW)

        ahead = [scores(i) for i in range(min(depth, ib))]
        for i in range(ib):
            s = ahead.pop(0)
            if i + depth < ib:
                ahead.append(scores(i + depth))
            eb = soft(s)
            e_s[i * kx : (i + 1) * kx] = eb
            v = kv_s[i * kx : (i + 1) * kx, c:]
            rows = slice(i * quarter, (i + 1) * quarter)
            o = dot_tn(eb, jnp.concatenate([v, ones], axis=1))
            o_s[rows, :] = pick(o[:, :c])
            r_s[rows, :] = 1.0 / pick(o[:, c:])

    for index, kx in enumerate(variants):
        low = variants[index - 1] if index else 0

        @pl.when(jnp.logical_and(length > low, length <= kx))
        def _():
            forward(kx)

    def middle_part(t, _):
        rows = pl.ds(pl.multiple_of(t * tb, tb), tb)
        per = tb // quarter
        block = pl.ds(t * per, per)
        rinv = r_s[rows, :]
        blended = o_s[rows, :] * rinv
        gate = g_s[rows, :]
        gated = (gate * blended).astype(LOW)
        gated_s[rows, :] = gated
        mid = xq_ref[0, block].reshape(tb, c).astype(FULL) + dot_nn(gated, wo_ref[...])
        n2, spread = normalize(mid)
        shaped = (n2 * g2 + g3).astype(LOW)
        sh_s[rows, :] = shaped
        hp = dot_nn(shaped, up_ref[...])
        sg = 0.5 * jnp.tanh(0.5 * hp) + 0.5
        silu = hp * sg
        hid = silu.astype(LOW)
        hid_s[rows, :] = hid
        res_ref[0, block] = (mid + dot_nn(hid, down_ref[...])).astype(LOW).reshape(per, quarter, c)
        cot = cot_ref[0, block].reshape(tb, c)
        dh = dot_nt(cot, down_ref[...])
        dpre = (dh * (sg + silu * (1.0 - sg))).astype(LOW)
        dpre_s[rows, :] = dpre
        dsh = dot_nt(dpre, up_ref[...])
        ggain_ref[2:3, :] += jnp.sum(dsh * n2, axis=0, keepdims=True)
        ggain_ref[3:4, :] += jnp.sum(dsh, axis=0, keepdims=True)
        u = dsh * g2
        first = jnp.mean(u, axis=-1, keepdims=True)
        second = jnp.mean(u * n2, axis=-1, keepdims=True)
        dmid = cot.astype(FULL) + spread * (u - first - n2 * second)
        dml = dmid.astype(LOW)
        dml_s[rows, :] = dml
        dmid_ref[0, block] = dml.reshape(per, quarter, c)
        dgated = dot_nt(dml, wo_ref[...])
        dblend = dgated * gate
        dqg_s[rows, c:] = (dblend * blended * (1.0 - gate)).astype(LOW)
        dos = (dblend * rinv).astype(LOW)
        dos_s[block] = dos.reshape(per, quarter, c)
        xn_s[block] = (-dos.astype(FULL) * blended).astype(LOW).reshape(per, quarter, c)
        return 0

    lax.fori_loop(0, tokens // tb, middle_part, 0)
    cot_all = cot_ref[0].reshape(tokens, c)
    gdown_ref[...] += dot_tn(cot_all, hid_s[...])
    gup_ref[...] += dot_tn(sh_s[...], dpre_s[...])
    gout_ref[...] += dot_tn(gated_s[...], dml_s[...])

    def backward(kx):
        ones = jnp.ones((kx, c), LOW)

        def d_scores(i):
            dbd = block_diag(dos_s[i])
            xbd = block_diag(xn_s[i])
            v_one = jnp.concatenate([kv_s[i * kx : (i + 1) * kx, c:], ones], axis=1)
            return dot_nt(v_one, jnp.concatenate([dbd, xbd], axis=1)), dbd

        ahead = [d_scores(i) for i in range(min(depth, ib))]
        for i in range(ib):
            dp, dbd = ahead.pop(0)
            if i + depth < ib:
                ahead.append(d_scores(i + depth))
            span = slice(i * kx, (i + 1) * kx)
            qbd = block_diag(q_s[i])
            eb = e_s[span]
            dl = eb.astype(FULL) * dp
            dbias_s[:kx, :] += dl
            dlb = dl.astype(LOW)
            dkv_s[span, c:] = dot_nn(eb, dbd).astype(LOW)
            dkv_s[span, :c] = (dot_nn(dlb, qbd) * LN2).astype(LOW)
            k = kv_s[span, :c]
            dq = pick(dot_tn(dlb, k))
            dqg_s[i * quarter : (i + 1) * quarter, :c] = (dq * score).astype(LOW)
        dkv = dkv_s[: ib * kx]
        gkv_ref[...] += dot_tn(n_s[: ib * kx], dkv)
        dn_s[:, :kx, :] = dot_nt(dkv, wkv_ref[...]).reshape(ib, kx, c)
        if kx < res:
            dn_s[:, kx:, :] = jnp.zeros((ib, res - kx, c), FULL)

    for index, kx in enumerate(variants):
        low = variants[index - 1] if index else 0

        @pl.when(jnp.logical_and(length > low, length <= kx))
        def _():
            backward(kx)

    own = pl.ds(pl.multiple_of(q * quarter, quarter), quarter)
    dn_s[:, own, :] += dot_nt(dqg_s[...], wqg_ref[...]).reshape(ib, quarter, c)
    y = q // 2
    k = q % 2
    for rel in range(2):
        yy = y if rel == 0 else 1 - y
        keep = pl.ds(pl.multiple_of((yy * 2 + k) * quarter, quarter), quarter)
        send = pl.ds(pl.multiple_of((yy * 2 + 1 - k) * quarter, quarter), quarter)
        (own0_ref, own1_ref)[rel][0] = dn_s[:, keep, :].astype(LOW)
        (sib0_ref, sib1_ref)[rel][0] = dn_s[:, send, :].astype(LOW)
    gqg_ref[...] += dot_tn(nq_s[...], dqg_s[...])

    @pl.when(blk == pl.num_programs(1) - 1)
    def _():
        for g in range(quarter // rl):
            dbias_ref[0, g] = dbias_s[:, g * heads * rl : (g + 1) * heads * rl].astype(LOW)


def main_call(start, count, lengths, qidx, pair_rep, cot, bias, weights, grads, carried=(), after=(), *, ib=8, variants=(128, 192, 256), tb=512, depth=2):
    wkv, wqg, wo, up, down, gains = weights
    items, rl, res, c = pair_rep.shape
    quarter = cot.shape[2]
    hid = up.shape[1]
    heads = 4
    width = c // heads
    ib = min(ib, rl)
    tokens = ib * quarter
    hj = heads * quarter
    grid = (count, rl // ib)

    def whole(shape):
        return pl.BlockSpec(shape, lambda b, i, *_: (0,) * len(shape))

    x_spec = pl.BlockSpec((1, ib, res, c), lambda b, i, ln, q: (start + b, i, 0, 0))
    xq_spec = pl.BlockSpec((1, ib, quarter, c), lambda b, i, ln, q: (start + b, i, q[0], 0))
    cot_spec = pl.BlockSpec((1, ib, quarter, c), lambda b, i, ln, q: (start + b, i, 0, 0))
    out_q = pl.BlockSpec((1, ib, quarter, c), lambda b, i, ln, q: (b, i, 0, 0))
    bias_spec = pl.BlockSpec((1,) + bias.shape[1:], lambda b, i, ln, q: (start + b, 0, 0, 0))
    grad_shapes = [(c, 2 * c), (c, 2 * c), (c, c), (c, hid), (c, hid), (8, c)]
    kern = functools.partial(
        main_kernel, start=start, ib=ib, heads=heads, width=width, variants=variants, tb=tb, depth=depth, rl=rl
    )
    any_spec = pl.BlockSpec(memory_space=pl.ANY)
    part = jax.ShapeDtypeStruct((count, rl, quarter, c), LOW)
    return pl.pallas_call(
        kern,
        grid_spec=pltpu.PrefetchScalarGridSpec(
            num_scalar_prefetch=2,
            grid=grid,
            in_specs=[x_spec, xq_spec, cot_spec, bias_spec]
            + [whole(w.shape) for w in weights]
            + [whole(s) for s in grad_shapes]
            + [any_spec] * (len(carried) + len(after)),
            out_specs=[cot_spec] + [out_q] * 5 + [bias_spec] + [whole(s) for s in grad_shapes],
            scratch_shapes=[
                pltpu.VMEM((ib * res, c), LOW),
                pltpu.VMEM((ib * res, 2 * c), LOW),
                pltpu.VMEM((ib * res, 2 * c), LOW),
                pltpu.VMEM((ib * res, hj), LOW),
                pltpu.VMEM((tokens, c), LOW),
                pltpu.VMEM((ib, quarter, c), LOW),
                pltpu.VMEM((tokens, c), FULL),
                pltpu.VMEM((tokens, c), FULL),
                pltpu.VMEM((tokens, c), FULL),
                pltpu.VMEM((ib, quarter, c), LOW),
                pltpu.VMEM((ib, quarter, c), LOW),
                pltpu.VMEM((tokens, hid), LOW),
                pltpu.VMEM((tokens, hid), LOW),
                pltpu.VMEM((tokens, c), LOW),
                pltpu.VMEM((tokens, c), LOW),
                pltpu.VMEM((tokens, c), LOW),
                pltpu.VMEM((tokens, 2 * c), LOW),
                pltpu.VMEM((res, hj), FULL),
                pltpu.VMEM((res, hj), FULL),
                pltpu.VMEM((ib, res, c), FULL),
            ],
        ),
        out_shape=[jax.ShapeDtypeStruct((items, rl, quarter, c), LOW)]
        + [part] * 5
        + [jax.ShapeDtypeStruct(bias.shape, LOW)]
        + [jax.ShapeDtypeStruct(s, FULL) for s in grad_shapes],
        input_output_aliases={18: 0, 19: 6} if carried else {},
        compiler_params=pltpu.CompilerParams(
            dimension_semantics=("arbitrary", "arbitrary"), vmem_limit_bytes=56 * 1024 * 1024
        ),
        cost_estimate=pl.CostEstimate(
            flops=60_000_000 * count * rl * 8, bytes_accessed=2_000_000 * count * rl // 8, transcendentals=0
        ),
        name="layer",
    )(lengths, qidx, pair_rep, pair_rep, cot, bias, *weights, *grads, *carried, *after)


MESH = pl.DeviceIdType.MESH
MOMENTUM = 0.9
AVERAGE = 0.6
RATES = (0.5, 0.3, 3.0, 0.05, 0.03, 0.1)
CHUNKS = (4, 3, 3, 2)


def pad16(n):
    return -(-n // 16) * 16


def greet_all(n_dev, n_heads, me):
    barrier = pltpu.get_barrier_semaphore()

    def signal(s, _):
        d = lax.rem(me + s, n_dev)
        pl.semaphore_signal(barrier, inc=1, device_id=(d // n_heads, lax.rem(d, n_heads)), device_id_type=MESH)
        return 0

    lax.fori_loop(1, n_dev, signal, 0)
    pl.semaphore_wait(barrier, n_dev - 1)


def prep_kernel(
    x_hbm, proj_ref, bw_ref, out_ref, up_ref, down_ref, gains_ref,
    wkv_ref, wqg_ref, wo_ref, upall_ref, downall_ref, gainall_ref, base_ref, bias_hbm,
    stage, wbuf, proj_s, up_s, down_s, base_s, stack_ref, xbuf, xhat, pbuf,
    x_sem, wsend, wrecv, bsend, brecv, self_sem,
    *, n_rows, n_heads, parts,
):
    items, rl, res, c = x_hbm.shape
    hid = up_ref.shape[1]
    quarter = res // n_heads
    width = out_ref.shape[0]
    n_dev = n_rows * n_heads
    group = n_rows // n_heads
    lanes = n_heads * rl
    r = lax.axis_index("rows")
    q = lax.axis_index("heads")
    me = r * n_heads + q

    def load(b):
        span = pl.ds(pl.multiple_of(q * quarter, quarter), quarter)
        return pltpu.make_async_copy(x_hbm.at[b, :, span, :], xbuf.at[b], x_sem.at[b])

    for b in range(items):
        load(b).start()

    pr, ur, dr, cr, cd = c // n_rows, c // n_dev, hid // n_dev, c // n_rows, c // n_dev
    o_down = pad16(pr)
    o_up = o_down + pad16(dr)
    o_out = o_up + pad16(ur * (hid // c))
    o_gain = o_out + pad16(width)
    o_bias = o_gain + 16
    lane = lax.broadcasted_iota(jnp.int32, (1, c), 1)
    stage[...] = jnp.zeros_like(stage)
    stage[:pr, :] = proj_ref[...]
    stage[o_down : o_down + dr, :] = down_ref[...]
    for g in range(hid // c):
        stage[o_up + g * ur : o_up + (g + 1) * ur, :] = up_ref[:, g * c : (g + 1) * c]
    placed = jnp.zeros((width, c), FULL)
    for i in range(cr):
        placed = placed + jnp.where(lane == r * cr + i, out_ref[:, i : i + 1], 0.0)
    stage[o_out : o_out + width, :] = placed
    placed = jnp.zeros((4, c), FULL)
    for i in range(cd):
        placed = placed + jnp.where(lane == me * cd + i, gains_ref[:, i : i + 1], 0.0)
    stage[o_gain : o_gain + 4, :] = placed
    stage[o_bias : o_bias + pr, :] = jnp.where(lane // rl == q, bw_ref[...], 0.0)
    wbuf[me] = stage[...].astype(LOW)

    greet_all(n_dev, n_heads, me)

    def weights_to(s):
        d = lax.rem(me + s, n_dev)
        return pltpu.make_async_remote_copy(
            src_ref=wbuf.at[me],
            dst_ref=wbuf.at[me],
            send_sem=wsend.at[s],
            recv_sem=wrecv.at[s],
            device_id=(d // n_heads, lax.rem(d, n_heads)),
            device_id_type=MESH,
        )

    def start_one(s, _):
        weights_to(s).start()
        return 0

    lax.fori_loop(1, n_dev, start_one, 0)

    for b in range(items):
        load(b).wait()
        xhat[b] = normalize(xbuf[b].reshape(rl * quarter, c).astype(FULL))[0]

    def wait_one(s, _):
        weights_to(s).wait()
        return 0

    lax.fori_loop(1, n_dev, wait_one, 0)

    gain_sum = jnp.zeros((16, c), FULL)
    for h in range(n_heads):
        whole = jnp.zeros((width, c), FULL)
        for rr in range(n_rows):
            d = rr * n_heads + h
            proj_s[rr * pr : (rr + 1) * pr, h * c : (h + 1) * c] = wbuf[d, :pr].astype(FULL)
            whole = whole + wbuf[d, o_out : o_out + width].astype(FULL)
        wo_ref[h * width : (h + 1) * width, :] = whole.astype(LOW)
    for d in range(n_dev):
        down_s[d * dr : (d + 1) * dr, :] = wbuf[d, o_down : o_down + dr].astype(FULL)
        for g in range(hid // c):
            up_s[d * ur : (d + 1) * ur, g * c : (g + 1) * c] = wbuf[d, o_up + g * ur : o_up + (g + 1) * ur].astype(FULL)
        gain_sum = gain_sum + wbuf[d, o_gain : o_gain + 16].astype(FULL)
    for rr in range(n_rows):
        total = jnp.zeros((pr, c), FULL)
        for h in range(n_heads):
            total = total + wbuf[rr * n_heads + h, o_bias : o_bias + pr].astype(FULL)
        base_s[rr * pr : (rr + 1) * pr, :] = total
    downall_ref[...] = down_s[...].astype(LOW)
    upall_ref[...] = up_s[...].astype(LOW)
    gainall_ref[...] = gain_sum[:8]
    src = lax.broadcasted_iota(jnp.int32, (n_heads * c, 2 * c), 0)
    dst = lax.broadcasted_iota(jnp.int32, (n_heads * c, 2 * c), 1)
    place = (lax.rem(dst, c) // width) * c + lax.rem(dst, width)
    second = dst // c
    proj_low = proj_s[...].astype(LOW)
    wqg_ref[...] = dot_nn(proj_low, (src == place + second * 3 * width).astype(LOW)).astype(LOW)
    wkv_ref[...] = dot_nn(proj_low, (src == place + width + second * width).astype(LOW)).astype(LOW)
    base = base_s[...]
    base_ref[...] = base[:, :lanes].astype(LOW)
    for jj in range(rl):
        stack_ref[jj * c : (jj + 1) * c, :] = jnp.where(lax.rem(lane, rl) == jj, base, 0.0)[:, :lanes].astype(LOW)

    g0 = gain_sum[0:1]
    g1 = gain_sum[1:2]
    target = r // group
    slot = lax.rem(r, group)
    span = pl.ds(pl.multiple_of(q * quarter, quarter), quarter)
    size = items // parts

    def own_copy(p):
        return pltpu.make_async_copy(
            pbuf.at[pl.ds(p * size, size)], bias_hbm.at[pl.ds(p * size, size), slot, span, :], self_sem.at[p]
        )

    def bias_to(p, t, s):
        return pltpu.make_async_remote_copy(
            src_ref=pbuf.at[pl.ds(p * size, size)],
            dst_ref=bias_hbm.at[pl.ds(p * size, size), slot, span, :],
            send_sem=bsend.at[p, t],
            recv_sem=brecv.at[p, s],
            device_id=(t, target),
            device_id_type=MESH,
        )

    mine = slot * n_heads + q
    for p in range(parts):

        def piece(b, _):
            n = (xhat[b] * g0 + g1).astype(LOW).reshape(rl, quarter, c)
            wide = jnp.concatenate([n[jj] for jj in range(rl)], axis=1)
            pbuf[b] = dot_nn(wide, stack_ref[...]).astype(LOW)
            return 0

        lax.fori_loop(p * size, (p + 1) * size, piece, 0)

        def send(t, _):
            is_me = jnp.logical_and(t == r, target == q)

            @pl.when(is_me)
            def _():
                own_copy(p).start()

            @pl.when(jnp.logical_not(is_me))
            def _():
                bias_to(p, t, mine).start()

            return 0

        lax.fori_loop(0, n_rows, send, 0)

    for p in range(parts):

        def finish(t, _):
            is_me = jnp.logical_and(t == r, target == q)

            @pl.when(is_me)
            def _():
                own_copy(p).wait()

            @pl.when(jnp.logical_not(is_me))
            def _():
                bias_to(p, t, mine).wait_send()

            from_me = jnp.logical_and(q * group + t // n_heads == r, lax.rem(t, n_heads) == q)

            @pl.when(jnp.logical_not(from_me))
            def _():
                bias_to(p, t, t).wait_recv()

            return 0

        lax.fori_loop(0, n_rows, finish, 0)


def prep_call(pair_rep, weights, n_rows, n_heads, quarter, parts=3):
    items, rl, res, c = pair_rep.shape
    proj, bw, out, up, down, gains = weights
    hid = up.shape[1]
    n_dev = n_rows * n_heads
    group = n_rows // n_heads
    lanes = n_heads * rl
    width = out.shape[0]
    rows = pad16(c // n_rows) + pad16(hid // n_dev) + pad16(c // n_dev * (hid // c)) + pad16(width) + 16 + pad16(c // n_rows)
    vmem = pl.BlockSpec(memory_space=pltpu.VMEM)
    hbm = pl.BlockSpec(memory_space=pl.ANY)
    return pl.pallas_call(
        functools.partial(prep_kernel, n_rows=n_rows, n_heads=n_heads, parts=parts),
        in_specs=[hbm] + [vmem] * 6,
        out_specs=[vmem] * 7 + [hbm],
        out_shape=[
            jax.ShapeDtypeStruct((c, 2 * c), LOW),
            jax.ShapeDtypeStruct((c, 2 * c), LOW),
            jax.ShapeDtypeStruct((c, c), LOW),
            jax.ShapeDtypeStruct((c, hid), LOW),
            jax.ShapeDtypeStruct((hid, c), LOW),
            jax.ShapeDtypeStruct((8, c), FULL),
            jax.ShapeDtypeStruct((c, lanes), LOW),
            jax.ShapeDtypeStruct((items, group, res, lanes), LOW),
        ],
        scratch_shapes=[
            pltpu.VMEM((rows, c), FULL),
            pltpu.VMEM((n_dev, rows, c), LOW),
            pltpu.VMEM((c, n_heads * c), FULL),
            pltpu.VMEM((c, hid), FULL),
            pltpu.VMEM((hid, c), FULL),
            pltpu.VMEM((c, c), FULL),
            pltpu.VMEM((rl * c, lanes), LOW),
            pltpu.VMEM((items, rl, quarter, c), LOW),
            pltpu.VMEM((items, rl * quarter, c), FULL),
            pltpu.VMEM((items, quarter, lanes), LOW),
            pltpu.SemaphoreType.DMA((items,)),
            pltpu.SemaphoreType.DMA((n_dev,)),
            pltpu.SemaphoreType.DMA((n_dev,)),
            pltpu.SemaphoreType.DMA((parts, n_rows)),
            pltpu.SemaphoreType.DMA((parts, n_rows)),
            pltpu.SemaphoreType.DMA((parts,)),
        ],
        compiler_params=pltpu.CompilerParams(
            collective_id=0, has_side_effects=True, vmem_limit_bytes=56 * 1024 * 1024
        ),
        name="prep",
    )(pair_rep, *weights)


def gather_kernel(
    grads_hbm, dbias_hbm, near_hbm, far_hbm, diagonal_hbm, sums_ref, db_ref,
    gbuf, dbuf, gsend, grecv, dsend, drecv, self_sem,
    *, n_rows, n_heads,
):
    n_dev = n_rows * n_heads
    group = n_rows // n_heads
    items, _, res, lanes = dbias_hbm.shape
    quarter = res // n_heads
    r = lax.axis_index("rows")
    q = lax.axis_index("heads")
    me = r * n_heads + q
    greet_all(n_dev, n_heads, me)

    def db_src(g, h):
        return dbias_hbm.at[:, g, pl.ds(pl.multiple_of(h * quarter, quarter), quarter), :]

    def db_to(t):
        g, h = t // n_heads, lax.rem(t, n_heads)
        return pltpu.make_async_remote_copy(
            src_ref=db_src(g, h),
            dst_ref=dbuf.at[r],
            send_sem=dsend.at[t],
            recv_sem=drecv.at[r],
            device_id=(q * group + g, h),
            device_id_type=MESH,
        )

    def db_from(t):
        return pltpu.make_async_remote_copy(
            src_ref=dbuf.at[t],
            dst_ref=dbuf.at[t],
            send_sem=dsend.at[t],
            recv_sem=drecv.at[t],
            device_id=(t, q),
            device_id_type=MESH,
        )

    def db_own(t):
        return pltpu.make_async_copy(db_src(t // n_heads, lax.rem(t, n_heads)), dbuf.at[r], self_sem.at[0])

    def is_me(t):
        return jnp.logical_and(q * group + t // n_heads == r, lax.rem(t, n_heads) == q)

    def from_me(t):
        return jnp.logical_and(t == r, r // group == q)

    def db_start(t, _):
        @pl.when(is_me(t))
        def _():
            db_own(t).start()

        @pl.when(jnp.logical_not(is_me(t)))
        def _():
            db_to(t).start()

        return 0

    lax.fori_loop(0, n_rows, db_start, 0)

    def grad_to(s):
        d = lax.rem(me + s, n_dev)
        return pltpu.make_async_remote_copy(
            src_ref=grads_hbm.at[d],
            dst_ref=gbuf.at[me],
            send_sem=gsend.at[s],
            recv_sem=grecv.at[s],
            device_id=(d // n_heads, lax.rem(d, n_heads)),
            device_id_type=MESH,
        )

    def grad_start(s, _):
        grad_to(s).start()
        return 0

    lax.fori_loop(1, n_dev, grad_start, 0)
    own = pltpu.make_async_copy(grads_hbm.at[me], gbuf.at[me], self_sem.at[1])
    own.start()
    own.wait()

    def grad_wait(s, _):
        grad_to(s).wait()
        return 0

    lax.fori_loop(1, n_dev, grad_wait, 0)

    def grad_add(d, total):
        return total + gbuf[d].astype(FULL)

    sums_ref[...] = lax.fori_loop(0, n_dev, grad_add, jnp.zeros(sums_ref.shape, FULL))

    def db_wait(t, _):
        @pl.when(is_me(t))
        def _():
            db_own(t).wait()

        @pl.when(jnp.logical_not(is_me(t)))
        def _():
            db_to(t).wait_send()

        @pl.when(jnp.logical_not(from_me(t)))
        def _():
            db_from(t).wait_recv()

        return 0

    lax.fori_loop(0, n_rows, db_wait, 0)

    def db_add(b, _):
        total = jnp.zeros((quarter, lanes), FULL)
        for t in range(n_rows):
            total = total + dbuf[t, b].astype(FULL)
        db_ref[b] = total.astype(LOW)
        return 0

    lax.fori_loop(0, items, db_add, 0)


def gather_call(grads, dbias, after, n_rows, n_heads):
    n_dev = n_rows * n_heads
    items, group, res, lanes = dbias.shape
    quarter = res // n_heads
    rows, c = grads.shape[1:]
    vmem = pl.BlockSpec(memory_space=pltpu.VMEM)
    hbm = pl.BlockSpec(memory_space=pl.ANY)
    return pl.pallas_call(
        functools.partial(gather_kernel, n_rows=n_rows, n_heads=n_heads),
        in_specs=[hbm] * 5,
        out_specs=[vmem, vmem],
        out_shape=[
            jax.ShapeDtypeStruct((rows, c), FULL),
            jax.ShapeDtypeStruct((items, quarter, lanes), LOW),
        ],
        scratch_shapes=[
            pltpu.VMEM((n_dev, rows, c), LOW),
            pltpu.VMEM((n_rows, items, quarter, lanes), LOW),
            pltpu.SemaphoreType.DMA((n_dev,)),
            pltpu.SemaphoreType.DMA((n_dev,)),
            pltpu.SemaphoreType.DMA((n_rows,)),
            pltpu.SemaphoreType.DMA((n_rows,)),
            pltpu.SemaphoreType.DMA((2,)),
        ],
        compiler_params=pltpu.CompilerParams(
            collective_id=1, has_side_effects=True, vmem_limit_bytes=56 * 1024 * 1024
        ),
        name="gather",
    )(grads, dbias, *after)


def small_kernel(ggain_ref, gbias_ref, sums_ref, buf, send_sem, recv_sem, *, n_rows, n_heads):
    n_dev = n_rows * n_heads
    lanes = gbias_ref.shape[1]
    rl = lanes // n_heads
    r = lax.axis_index("rows")
    q = lax.axis_index("heads")
    me = r * n_heads + q
    heads = lax.broadcasted_iota(jnp.int32, (8, lanes), 0) - 2
    sel = (lax.broadcasted_iota(jnp.int32, (8, lanes), 1) // rl == heads).astype(FULL)
    rows = lax.dot_general(
        sel, gbias_ref[...], (((1,), (1,)), ((), ())), precision=lax.Precision.HIGHEST, preferred_element_type=FULL
    )
    row = lax.broadcasted_iota(jnp.int32, ggain_ref.shape, 0)
    buf[me] = jnp.where(row < 2, ggain_ref[...], rows)
    greet_all(n_dev, n_heads, me)

    def copy_to(s):
        d = lax.rem(me + s, n_dev)
        return pltpu.make_async_remote_copy(
            src_ref=buf.at[me],
            dst_ref=buf.at[me],
            send_sem=send_sem.at[s],
            recv_sem=recv_sem.at[s],
            device_id=(d // n_heads, lax.rem(d, n_heads)),
            device_id_type=MESH,
        )

    def start_one(s, _):
        copy_to(s).start()
        return 0

    def wait_one(s, _):
        copy_to(s).wait()
        return 0

    lax.fori_loop(1, n_dev, start_one, 0)
    lax.fori_loop(1, n_dev, wait_one, 0)
    sums_ref[...] = lax.fori_loop(0, n_dev, lambda d, t: t + buf[d], jnp.zeros(sums_ref.shape, FULL))


def small_call(ggain, gbias, n_rows, n_heads):
    n_dev = n_rows * n_heads
    vmem = pl.BlockSpec(memory_space=pltpu.VMEM)
    return pl.pallas_call(
        functools.partial(small_kernel, n_rows=n_rows, n_heads=n_heads),
        in_specs=[vmem, vmem],
        out_specs=vmem,
        out_shape=jax.ShapeDtypeStruct(ggain.shape, FULL),
        scratch_shapes=[
            pltpu.VMEM((n_dev,) + ggain.shape, FULL),
            pltpu.SemaphoreType.DMA((n_dev,)),
            pltpu.SemaphoreType.DMA((n_dev,)),
        ],
        compiler_params=pltpu.CompilerParams(collective_id=2, has_side_effects=True),
        name="small",
    )(ggain, gbias)


def norm_back(d_hat, normal, spread):
    first = jnp.mean(d_hat, axis=-1, keepdims=True)
    second = jnp.mean(d_hat * normal, axis=-1, keepdims=True)
    return spread * (d_hat - first - normal * second)


def final_kernel(
    q_ref, x_ref, dmid_ref, own_ref, a_ref, b_ref, c_ref, db_ref, gain_ref, base_ref, gin_ref, bin_ref, *rest,
):
    out_ref, ggain_ref, gbias_ref = rest[-3:]
    _, rl, quarter, c = x_ref.shape
    tokens = rl * quarter
    lanes = db_ref.shape[2]

    @pl.when(pl.program_id(0) == 0)
    def _():
        ggain_ref[...] = gin_ref[...]
        gbias_ref[...] = bin_ref[...]

    g0 = gain_ref[0:1, :]
    normal, spread = normalize(x_ref[0].reshape(tokens, c).astype(FULL))
    normed = (normal * g0 + gain_ref[1:2, :]).astype(LOW)
    db = db_ref[0]
    lane = lax.rem(lax.broadcasted_iota(jnp.int32, (1, lanes), 1), rl)
    spread_db = jnp.concatenate([jnp.where(lane == jj, db, jnp.zeros_like(db)) for jj in range(rl)], axis=0)
    gbias_ref[...] += dot_tn(normed, spread_db)
    total = own_ref[0].astype(FULL) + a_ref[0].astype(FULL) + b_ref[0].astype(FULL) + c_ref[0].astype(FULL)
    dn = total.reshape(tokens, c) + dot_nt(spread_db, base_ref[...])
    ggain_ref[0:1, :] += jnp.sum(dn * normal, axis=0, keepdims=True)
    ggain_ref[1:2, :] += jnp.sum(dn, axis=0, keepdims=True)
    back = norm_back(dn * g0, normal, spread)
    out_ref[0] = (dmid_ref[0].astype(FULL) + back.reshape(rl, quarter, c)).astype(LOW)


def final_call(qidx, pair_rep, terms, db, gains, base, sums, start, carried=()):
    items, rl, res, c = pair_rep.shape
    count, _, quarter, _ = terms[0].shape
    lanes = db.shape[2]
    one = pl.BlockSpec((1, rl, quarter, c), lambda b, q: (b, 0, 0, 0))
    small = pl.BlockSpec((8, c), lambda b, q: (0, 0))
    wide = pl.BlockSpec((c, lanes), lambda b, q: (0, 0))
    return pl.pallas_call(
        final_kernel,
        grid_spec=pltpu.PrefetchScalarGridSpec(
            num_scalar_prefetch=1,
            grid=(count,),
            in_specs=[pl.BlockSpec((1, rl, quarter, c), lambda b, q: (start + b, 0, q[0], 0))]
            + [one] * 5
            + [pl.BlockSpec((1, quarter, lanes), lambda b, q: (start + b, 0, 0)), small]
            + [wide, small, wide]
            + [pl.BlockSpec(memory_space=pl.ANY)] * len(carried),
            out_specs=[pl.BlockSpec((1, rl, quarter, c), lambda b, q: (start + b, 0, 0, 0)), small, wide],
        ),
        out_shape=[
            jax.ShapeDtypeStruct((items, rl, quarter, c), LOW),
            jax.ShapeDtypeStruct((8, c), FULL),
            jax.ShapeDtypeStruct((c, lanes), FULL),
        ],
        input_output_aliases={12: 0} if carried else {},
        compiler_params=pltpu.CompilerParams(vmem_limit_bytes=56 * 1024 * 1024),
        name="last",
    )(qidx, pair_rep, *terms, db, gains, base, *sums, *carried)


def update(weight, gradient, moment, average, step_rate, root_pairs):
    moment_next = MOMENTUM * moment + gradient
    weight_next = weight - step_rate / root_pairs * (gradient + MOMENTUM * moment_next)
    return (weight_next, moment_next, AVERAGE * average + (1.0 - AVERAGE) * weight_next)


def shards(
    pair_rep, lengths,
    proj_weight, bias_weight, out_weight, up_weight, down_weight, norm_gains,
    proj_moment, bias_moment, out_moment, up_moment, down_moment, gains_moment,
    proj_average, bias_average, out_average, up_average, down_average, gains_average,
    cotangent,
    *, n_rows, n_heads,
):
    both = ("rows", "heads")
    items, rl, res, c = pair_rep.shape
    quarter = cotangent.shape[2]
    hid = up_weight.shape[1]
    width = out_weight.shape[0]
    n_dev = n_rows * n_heads
    q = lax.axis_index("heads").astype(jnp.int32)
    r = lax.axis_index("rows").astype(jnp.int32)
    qidx = q.reshape(1)
    weights = (proj_weight, bias_weight, out_weight, up_weight, down_weight, norm_gains)
    wkv, wqg, wo, up, down, gains, base, bias = prep_call(pair_rep, weights, n_rows, n_heads, quarter)

    core = [(d, d ^ 1) for d in range(n_dev)]
    cross = [(d, d ^ 2) for d in range(n_dev)]
    both_moved = [(d, d ^ 3) for d in range(n_dev)]

    grads = [jnp.zeros(s, FULL) for s in [(c, 2 * c), (c, 2 * c), (c, c), (c, hid), (c, hid), (8, c)]]
    carried = ()
    terms = []
    start = 0
    for count in CHUNKS:
        outs = main_call(
            start, count, lengths, qidx, pair_rep, cotangent, bias, (wkv, wqg, wo, up, down, gains), grads, carried,
            terms[-2][1][2:] if len(terms) > 1 else (),
        )
        result, dmid, own0, own1, sib0, sib1, dbias = outs[:7]
        grads = list(outs[7:])
        carried = (result, dbias)
        far = lax.ppermute(own1, both, cross)
        diagonal = lax.ppermute(sib1, both, both_moved)
        near = lax.ppermute(sib0, both, core)
        terms.append((start, (dmid, own0, near, far, diagonal)))
        start += count

    gkv, gqg, gout, gup, gdown, gtwo = grads
    gproj = jnp.stack([gqg[:, :c], gkv[:, :c], gkv[:, c:], gqg[:, c:]]).reshape(4, c, n_heads, width)
    gproj = gproj.transpose(1, 2, 0, 3).reshape(n_rows, c // n_rows, n_heads, 4 * width).transpose(0, 2, 1, 3)
    go = gout.reshape(n_heads, width, n_rows, c // n_rows).transpose(2, 0, 1, 3)
    gg = gtwo[2:4].reshape(2, n_dev, c // n_dev).transpose(1, 0, 2)
    flat = [g.reshape(n_dev, -1).astype(LOW) for g in (gproj, go, gup, gdown.T, gg)]
    sizes = [g.shape[1] for g in flat]
    offs = [sum(sizes[:i]) for i in range(len(sizes))]
    full = -(-sum(sizes) // (16 * c)) * 16 * c
    flat = jnp.pad(jnp.concatenate(flat, axis=1), ((0, 0), (0, full - sum(sizes))))
    flat, db = gather_call(flat.reshape(n_dev, full // c, c), dbias, terms[-2][1][2:], n_rows, n_heads)
    flat = flat.reshape(-1)
    s_proj, s_out, s_up, s_down, s_two = [flat[o : o + s] for o, s in zip(offs, sizes)]

    sums = (jnp.zeros((8, c), FULL), jnp.zeros((c, n_heads * rl), FULL))
    done = ()
    for start, parts in terms:
        d_pair, *sums = final_call(qidx, pair_rep, parts, db, gains, base, sums, start, done)
        done = (d_pair,)
    small = small_call(*sums, n_rows, n_heads)
    cd, cr = c // n_dev, c // n_rows
    s_one = lax.dynamic_slice(small, (0, (r * n_heads + q) * cd), (2, cd))
    s_bias = lax.dynamic_slice(small, (2 + q, r * cr), (1, cr)).reshape(cr, 1)
    s_gains = jnp.concatenate([s_one, s_two.reshape(2, cd)])
    sums = (s_proj, s_bias, s_out, s_up, s_down, s_gains)
    moments = (proj_moment, bias_moment, out_moment, up_moment, down_moment, gains_moment)
    averages = (proj_average, bias_average, out_average, up_average, down_average, gains_average)
    root_pairs = math.sqrt(items * res * res)
    nexts = [
        update(w, g.reshape(w.shape), m, a, rate, root_pairs)
        for w, g, m, a, rate in zip(weights, sums, moments, averages, RATES)
    ]
    return (
        result,
        d_pair,
        *[n[0] for n in nexts],
        *[n[1] for n in nexts],
        *[n[2] for n in nexts],
    )


def solution(mesh):
    weight_specs = (
        P("rows", "heads"),
        P("rows", "heads"),
        P("heads", "rows"),
        P(("rows", "heads"), None),
        P(("rows", "heads"), None),
        P(None, ("rows", "heads")),
    )
    quarter_spec = P(None, "rows", "heads", None)
    in_specs = (P(None, "rows", None, None), P()) + weight_specs * 3 + (quarter_spec,)
    out_specs = (quarter_spec, quarter_spec) + weight_specs * 3
    body = functools.partial(shards, n_rows=mesh.shape["rows"], n_heads=mesh.shape["heads"])
    return jax.shard_map(body, mesh=mesh, in_specs=in_specs, out_specs=out_specs, check_vma=False)
```

time: 1070 us -> 595 us (0.56)
  waiting for transfers between devices: 424 us -> 28.4 us
  blocking collectives: 153 us -> 0 us
  Pallas kernels: 355 us -> 500 us
  local copies, waits for them, and re-layouts: 58.4 us -> 27.8 us
  other arithmetic: 35.9 us -> 8.44 us
  between operations: 15.1 us -> 1.54 us
    unnamed x8 -> x0, waiting for transfers between devices: 253 us -> none
    all_gather x4 -> x0, blocking collectives: 153 us -> none  [shards(): allb = lax.all_gather(piece, 'rows', axis=0, tiled=False)]
    pallas_call x4 -> x3, Pallas kernels: 17.9 us -> 159 us  [the longest x1 91.6 us: gather_call(): pl.pallas_call(functools.partial(gather_kernel, n_rows=n_rows, n_heads=n_...]
    reduce_scatter x4 -> x0, waiting for transfers between devices: 115 us -> none  [shards(): dbias = lax.psum_scatter(dbias, 'rows', scatter_dimension=0, tiled=False)]
    ppermute x20 -> x12, waiting for transfers between devices: 54.8 us -> 28.4 us  [the longest x4 28.4 us: shards(): diagonal = lax.ppermute(sib1, both, both_moved)]
    reshape x36 -> x2, local copies, waits for them, and re-layouts: 21 us -> 0.09 us  [shards(): g.reshape(w.shape)]
    concatenate x5 -> x0, other arithmetic: 13.9 us -> none  [the longest x1 6.18 us: shards(): jnp.concatenate(pairs, axis=0)]
    convert_element_type x6 -> x4, other arithmetic: 15.6 us -> 1.96 us  [shards(): g.reshape(n_dev, -1).astype(LOW)]
  transfers between devices with their start and end apart: 26 -> 12, of which waited for: 7 -> 2; matrix products, arithmetic and copies ran while one was open for 6% -> 4% of each run, Pallas kernels for 25% -> 56%
where the time goes in v2:
time: 595 us; the launch traced here: 586 us
  Pallas kernels  500 us (84%)
  waiting for transfers between devices  28.4 us (5%)
  local copies, waits for them, and re-layouts  27.8 us (5%)
  starting transfers between devices  19.9 us (3%)
  other arithmetic  8.44 us (1%)
    pallas_call x4, Pallas kernels, main_call(): pl.pallas_call(kern, grid_spec=pltpu.PrefetchScalarGridSpec(num_scalar_pr...  309 us
    pallas_call x1, Pallas kernels, gather_call(): pl.pallas_call(functools.partial(gather_kernel, n_rows=n_rows, n_heads=n_...  91.6 us
    pallas_call x1, Pallas kernels, prep_call(): pl.pallas_call(functools.partial(prep_kernel, n_rows=n_rows, n_heads=n_he...  52.4 us
    pallas_call x4, Pallas kernels, final_call(): pl.pallas_call(final_kernel, grid_spec=pltpu.PrefetchScalarGridSpec(num_s...  32.5 us
    ppermute x4, waiting for transfers between devices, shards(): diagonal = lax.ppermute(sib1, both, both_moved)  28.4 us
    ppermute x4, starting transfers between devices, shards(): far = lax.ppermute(own1, both, cross)  18.4 us
    pallas_call x1, Pallas kernels, small_call(): pl.pallas_call(functools.partial(small_kernel, n_rows=n_rows, n_heads=n_h...  15.3 us
  transfers between devices with their start and end apart: 12, of which 2 were waited for; matrix products, arithmetic and copies ran while one was open for 4% of the time, Pallas kernels for 56%

profile of v2, /device:TPU:0, one launch (start us, length us, event | category | flops | bytes accessed | tf_op | source)
XLA Modules:
  0.0 586.5 jit_solution(1149677514014149657)
XLA Ops:
  0.7 1.4 copy.75.out_ref
  2.0 1.3 copy.74.bw_ref
  3.4 52.4 %prep.1 = (bf16[128,256]{1,0:T(8,128)(2,1)}, bf16[128,256]{1,0:T(8,128)(2,1)}, bf16[128,128]{1,0:T(8,128)(2,1)}, bf16[128,512]{1,0:T(8,128)(2,1)}, bf16[512,128]...) custom-call(bf16[12,32,256,128]{3,2,1,0:T(8,128)(2,1)} %x_ref.15, ...), custom_call_target="tpu_custom_call" | custom-call | tf_op jit(solution)/shard_map/prep/pallas_call | solution.py:536
  58.4 99.8 %layer.4 = (bf16[12,32,64,128]{3,2,1,0:T(8,128)(2,1)}, bf16[4,32,64,128]{3,2,1,0:T(8,128)(2,1)}, bf16[4,32,64,128]{3,2,1,0:T(8,128)(2,1)}, bf16[4,32,64,128]{3,2...) custom-call(s32[12]{0:T(128)} %len_ref.7, ...), custom_call_target="tpu_custom_call" | custom-call | flops 61440000000 | bytes 32000000 | tf_op jit(solution)/shard_map/layer/pallas_call | solution.py:272
  158.4 13.1 %collective-permute-start.1 = (bf16[4,32,64,128]{3,2,1,0:T(8,128)(2,1)}, bf16[4,32,64,128]{3,2,1,0:T(8,128)(2,1)}, u32[]{:S(2)}, u32[]{:S(2)}) collective-permute-start(bf16[4,32,64,128]{3,2,1,0:T(8,128)(2,1)} %get-tuple-element.118), channel_id=1, source_target_pairs={{0,2},{1,3},{2,0},{3,1},{4,6},{5,7},{6,4},{7,5},{8,10},{9,11},{10,... | collective-permute-start | bytes 6291464 | tf_op jit(solution)/shard_map/ppermute | solution.py:888
  171.6 77.4 %layer.5 = (bf16[12,32,64,128]{3,2,1,0:T(8,128)(2,1)}, bf16[3,32,64,128]{3,2,1,0:T(8,128)(2,1)}, bf16[3,32,64,128]{3,2,1,0:T(8,128)(2,1)}, bf16[3,32,64,128]{3,2...) custom-call(s32[12]{0:T(128)} %len_ref.7, ...), custom_call_target="tpu_custom_call", output_to_operand_aliasing={{0}: (18, {}), {6}: (19, {})} | custom-call | flops 46080000000 | bytes 24000000 | tf_op jit(solution)/shard_map/layer/pallas_call | solution.py:272
  249.3 1.9 collective-permute-start.4
  252.0 10.8 %collective-permute-done.2.rest_4_.c_ref = bf16[4,32,64,128]{3,2,1,0:T(8,128)(2,1)} collective-permute-done((bf16[4,32,64,128]{3,2,1,0:T(8,128)(2,1)}, bf16[4,32,64,128]{3,2,1,0:T(8,128)(2,1)}, u32[]{:S(2)}, u32[]{:S(2)}) %collective-permute-start.2) | collective-permute-done | bytes 2097184 | tf_op jit(solution)/shard_map/ppermute | solution.py:889
  262.8 79.3 %layer.6 = (bf16[12,32,64,128]{3,2,1,0:T(8,128)(2,1)}, bf16[3,32,64,128]{3,2,1,0:T(8,128)(2,1)}, bf16[3,32,64,128]{3,2,1,0:T(8,128)(2,1)}, bf16[3,32,64,128]{3,2...) custom-call(s32[12]{0:T(128)} %len_ref.7, ...), custom_call_target="tpu_custom_call", output_to_operand_aliasing={{0}: (18, {}), {6}: (19, {})} | custom-call | flops 46080000000 | bytes 24000000 | tf_op jit(solution)/shard_map/layer/pallas_call | solution.py:272
  342.1 1.7 collective-permute-start.10
  343.8 1.2 copy-done.3
  344.9 52.2 %layer.7 = (bf16[12,32,64,128]{3,2,1,0:T(8,128)(2,1)}, bf16[2,32,64,128]{3,2,1,0:T(8,128)(2,1)}, bf16[2,32,64,128]{3,2,1,0:T(8,128)(2,1)}, bf16[2,32,64,128]{3,2...) custom-call(s32[12]{0:T(128)} %len_ref.7, ...), custom_call_target="tpu_custom_call", output_to_operand_aliasing={{0}: (18, {}), {6}: (19, {})} | custom-call | flops 30720000000 | bytes 16000000 | tf_op jit(solution)/shard_map/layer/pallas_call | solution.py:272
  400.2 1.1 copy.80
  401.3 1.4 convert_element_type.53
  404.7 1.0 convert_element_type.60
  405.8 1.0 convert_bitcast_fusion
  407.5 1.0 convert_element_type.64
  409.7 1.4 convert_element_type.65
  411.1 1.4 copy.85
  412.5 1.4 copy.86
  414.2 1.6 collective-permute-start.7
  418.4 17.6 %collective-permute-done.11.diagonal_hbm.c_ref = bf16[3,32,64,128]{3,2,1,0:T(8,128)(2,1)S(1)} collective-permute-done((bf16[3,32,64,128]{3,2,1,0:T(8,128)(2,1)}, bf16[3,32,64,128]{3,2,1,0:T(8,128)(2,1)S(1)}, u32[]{:S(2)}, u32[]{:S(2)}) %collective-permute-start.11) | collective-permute-done | bytes 1572896 | tf_op jit(solution)/shard_map/ppermute | solution.py:889
  436.0 1.1 copy-done.1
  437.2 91.6 %gather.1 = (f32[64,128]{1,0:T(8,128)}, bf16[12,64,128]{2,1,0:T(8,128)(2,1)}) custom-call(bf16[32,64,128]{2,1,0:T(8,128)(2,1)} %bitcast.35, bf16[12,2,256,128]{3,2,1,0:T(8,128)(2,1)} %get-tuple-element.143.dbias_hbm, bf16[3,32,64,128]{3,2,1,0:T(8,128)(2,1)} %collective-permute-done.9.near_hbm.a_ref, bf16[3,32,64,128]{3,2,1,0:T(8,128)(2,1)} %copy-done, ...), custom_call_target="tpu_custom_call" | custom-call | tf_op jit(solution)/shard_map/gather/pallas_call | solution.py:700
  528.7 1.8 slice.51
  533.4 1.4 multiply_add_fusion.2
  534.8 10.0 %last.4 = (bf16[12,32,64,128]{3,2,1,0:T(8,128)(2,1)}, f32[8,128]{1,0:T(8,128)}, f32[128,128]{1,0:T(8,128)}) custom-call(s32[1]{0:T(128)} %bitcast.q_ref, bf16[12,32,256,128]{3,2,1,0:T(8,128)(2,1)} %x_ref.15, bf16[4,32,64,128]{3,2,1,0:T(8,128)(2,1)} %get-tuple-element.153.dmid_ref, bf16[4,32,64,128]{3,2,1,0:T(8,128)(2,1)} %get-tuple-element.154.own_ref, ...), custom_call_target="tpu_custom_call" | custom-call | tf_op jit(solution)/shard_map/last/pallas_call | solution.py:823
  544.8 8.2 %last.5 = (bf16[12,32,64,128]{3,2,1,0:T(8,128)(2,1)}, f32[8,128]{1,0:T(8,128)}, f32[128,128]{1,0:T(8,128)}) custom-call(s32[1]{0:T(128)} %bitcast.q_ref, bf16[12,32,256,128]{3,2,1,0:T(8,128)(2,1)} %x_ref.15, bf16[3,32,64,128]{3,2,1,0:T(8,128)(2,1)} %get-tuple-element.151.dmid_ref, ...), custom_call_target="tpu_custom_call", output_to_operand_aliasing={{0}: (12, {})} | custom-call | tf_op jit(solution)/shard_map/last/pallas_call | solution.py:823
  553.0 8.1 %last.6 = (bf16[12,32,64,128]{3,2,1,0:T(8,128)(2,1)}, f32[8,128]{1,0:T(8,128)}, f32[128,128]{1,0:T(8,128)}) custom-call(s32[1]{0:T(128)} %bitcast.q_ref, bf16[12,32,256,128]{3,2,1,0:T(8,128)(2,1)} %x_ref.15, bf16[3,32,64,128]{3,2,1,0:T(8,128)(2,1)} %get-tuple-element.149.dmid_ref, ...), custom_call_target="tpu_custom_call", output_to_operand_aliasing={{0}: (12, {})} | custom-call | tf_op jit(solution)/shard_map/last/pallas_call | solution.py:823
  561.3 6.2 %last.7 = (bf16[12,32,64,128]{3,2,1,0:T(8,128)(2,1)}, f32[8,128]{1,0:T(8,128)}, f32[128,128]{1,0:T(8,128)}) custom-call(s32[1]{0:T(128)} %bitcast.q_ref, bf16[12,32,256,128]{3,2,1,0:T(8,128)(2,1)} %x_ref.15, bf16[2,32,64,128]{3,2,1,0:T(8,128)(2,1)} %get-tuple-element.132.dmid_ref, ...), custom_call_target="tpu_custom_call", output_to_operand_aliasing={{0}: (12, {})} | custom-call | tf_op jit(solution)/shard_map/last/pallas_call | solution.py:823
  567.5 15.3 %small.1 = f32[8,128]{1,0:T(8,128)} custom-call(f32[8,128]{1,0:T(8,128)} %get-tuple-element.166.ggain_ref, f32[128,128]{1,0:T(8,128)} %get-tuple-element.167.gbias_ref), custom_call_target="tpu_custom_call" | custom-call | tf_op jit(solution)/shard_map/small/pallas_call | solution.py:767
  584.8 1.3 multiply_add_fusion.10
  (112 shorter events, 18.7 us)
Async XLA Ops:
  158.2 93.8 %collective-permute-start = (bf16[4,32,64,128]{3,2,1,0:T(8,128)(2,1)}, bf16[4,32,64,128]{3,2,1,0:T(8,128)(2,1)S(1)}, u32[]{:S(2)}, u32[]{:S(2)}) collective-permute-start(bf16[4,32,64,128]{3,2,1,0:T(8,128)(2,1)} %get-tuple-element.117), channel_id=1, source_target_pairs={{0,1},{1,0},{2,3},{3,2},{4,5},{5,4},{6,7},{7,6},{8,9},{9,8},{10,11... | collective-permute-start | bytes 6291464 | tf_op jit(solution)/shard_map/ppermute | solution.py:890
  158.4 93.6 %collective-permute-start.1 = (bf16[4,32,64,128]{3,2,1,0:T(8,128)(2,1)}, bf16[4,32,64,128]{3,2,1,0:T(8,128)(2,1)}, u32[]{:S(2)}, u32[]{:S(2)}) collective-permute-start(bf16[4,32,64,128]{3,2,1,0:T(8,128)(2,1)} %get-tuple-element.118), channel_id=1, source_target_pairs={{0,2},{1,3},{2,0},{3,1},{4,6},{5,7},{6,4},{7,5},{8,10},{9,11},{10,... | collective-permute-start | bytes 6291464 | tf_op jit(solution)/shard_map/ppermute | solution.py:888
  171.5 91.2 %collective-permute-start.2 = (bf16[4,32,64,128]{3,2,1,0:T(8,128)(2,1)}, bf16[4,32,64,128]{3,2,1,0:T(8,128)(2,1)}, u32[]{:S(2)}, u32[]{:S(2)}) collective-permute-start(bf16[4,32,64,128]{3,2,1,0:T(8,128)(2,1)} %get-tuple-element.119), channel_id=1, source_target_pairs={{0,3},{1,2},{2,1},{3,0},{4,7},{5,6},{6,5},{7,4},{8,11},{9,10},{10,... | collective-permute-start | bytes 6291464 | tf_op jit(solution)/shard_map/ppermute | solution.py:889
  171.6 79.6 %copy-start.13 = (f32[32,16]{0,1:T(8,128)S(1)}, f32[32,16]{0,1:T(8,128)}, u32[]{:S(2)}) copy-start(f32[32,16]{0,1:T(8,128)} %param.31) | copy-start | bytes 6148
  171.6 79.7 %copy-start.14 = (f32[32,16]{0,1:T(8,128)S(1)}, f32[32,16]{0,1:T(8,128)}, u32[]{:S(2)}) copy-start(f32[32,16]{0,1:T(8,128)} %param.37) | copy-start | bytes 6148
  249.1 94.7 %collective-permute-start.3 = (bf16[3,32,64,128]{3,2,1,0:T(8,128)(2,1)}, bf16[3,32,64,128]{3,2,1,0:T(8,128)(2,1)}, u32[]{:S(2)}, u32[]{:S(2)}) collective-permute-start(bf16[3,32,64,128]{3,2,1,0:T(8,128)(2,1)} %get-tuple-element.128), channel_id=1, source_target_pairs={{0,1},{1,0},{2,3},{3,2},{4,5},{5,4},{6,7},{7,6},{8,9},{9,8},{10,11... | collective-permute-start | bytes 4718600 | tf_op jit(solution)/shard_map/ppermute | solution.py:890
  249.3 94.5 %collective-permute-start.4 = (bf16[3,32,64,128]{3,2,1,0:T(8,128)(2,1)}, bf16[3,32,64,128]{3,2,1,0:T(8,128)(2,1)}, u32[]{:S(2)}, u32[]{:S(2)}) collective-permute-start(bf16[3,32,64,128]{3,2,1,0:T(8,128)(2,1)} %get-tuple-element.129), channel_id=1, source_target_pairs={{0,2},{1,3},{2,0},{3,1},{4,6},{5,7},{6,4},{7,5},{8,10},{9,11},{10,... | collective-permute-start | bytes 4718600 | tf_op jit(solution)/shard_map/ppermute | solution.py:888
  252.0 91.8 %collective-permute-start.5 = (bf16[3,32,64,128]{3,2,1,0:T(8,128)(2,1)}, bf16[3,32,64,128]{3,2,1,0:T(8,128)(2,1)S(1)}, u32[]{:S(2)}, u32[]{:S(2)}) collective-permute-start(bf16[3,32,64,128]{3,2,1,0:T(8,128)(2,1)} %get-tuple-element.130), channel_id=1, source_target_pairs={{0,3},{1,2},{2,1},{3,0},{4,7},{5,6},{6,5},{7,4},{8,11},{9,10},{10,... | collective-permute-start | bytes 4718600 | tf_op jit(solution)/shard_map/ppermute | solution.py:889
  342.1 74.5 %collective-permute-start.10 = (bf16[3,32,64,128]{3,2,1,0:T(8,128)(2,1)}, bf16[3,32,64,128]{3,2,1,0:T(8,128)(2,1)S(1)}, u32[]{:S(2)}, u32[]{:S(2)}) collective-permute-start(bf16[3,32,64,128]{3,2,1,0:T(8,128)(2,1)} %get-tuple-element.145), channel_id=1, source_target_pairs={{0,2},{1,3},{2,0},{3,1},{4,6},{5,7},{6,4},{7,5},{8,10},{9,11},{10,... | collective-permute-start | bytes 4718600 | tf_op jit(solution)/shard_map/ppermute | solution.py:888
  399.6 36.4 %collective-permute-start.11 = (bf16[3,32,64,128]{3,2,1,0:T(8,128)(2,1)}, bf16[3,32,64,128]{3,2,1,0:T(8,128)(2,1)S(1)}, u32[]{:S(2)}, u32[]{:S(2)}) collective-permute-start(bf16[3,32,64,128]{3,2,1,0:T(8,128)(2,1)} %get-tuple-element.146), channel_id=1, source_target_pairs={{0,3},{1,2},{2,1},{3,0},{4,7},{5,6},{6,5},{7,4},{8,11},{9,10},{10,... | collective-permute-start | bytes 4718600 | tf_op jit(solution)/shard_map/ppermute | solution.py:889
  400.0 35.9 %collective-permute-start.9 = (bf16[3,32,64,128]{3,2,1,0:T(8,128)(2,1)}, bf16[3,32,64,128]{3,2,1,0:T(8,128)(2,1)}, u32[]{:S(2)}, u32[]{:S(2)}) collective-permute-start(bf16[3,32,64,128]{3,2,1,0:T(8,128)(2,1)} %get-tuple-element.144), channel_id=1, source_target_pairs={{0,1},{1,0},{2,3},{3,2},{4,5},{5,4},{6,7},{7,6},{8,9},{9,8},{10,11... | collective-permute-start | bytes 4718600 | tf_op jit(solution)/shard_map/ppermute | solution.py:890
  413.8 147.3 %collective-permute-start.6 = (bf16[2,32,64,128]{3,2,1,0:T(8,128)(2,1)}, bf16[2,32,64,128]{3,2,1,0:T(8,128)(2,1)}, u32[]{:S(2)}, u32[]{:S(2)}) collective-permute-start(bf16[2,32,64,128]{3,2,1,0:T(8,128)(2,1)} %get-tuple-element.134), channel_id=1, source_target_pairs={{0,1},{1,0},{2,3},{3,2},{4,5},{5,4},{6,7},{7,6},{8,9},{9,8},{10,11... | collective-permute-start | bytes 3145736 | tf_op jit(solution)/shard_map/ppermute | solution.py:890
  414.2 147.0 %collective-permute-start.7 = (bf16[2,32,64,128]{3,2,1,0:T(8,128)(2,1)}, bf16[2,32,64,128]{3,2,1,0:T(8,128)(2,1)}, u32[]{:S(2)}, u32[]{:S(2)}) collective-permute-start(bf16[2,32,64,128]{3,2,1,0:T(8,128)(2,1)} %get-tuple-element.135), channel_id=1, source_target_pairs={{0,2},{1,3},{2,0},{3,1},{4,6},{5,7},{6,4},{7,5},{8,10},{9,11},{10,... | collective-permute-start | bytes 3145736 | tf_op jit(solution)/shard_map/ppermute | solution.py:888
  416.6 144.5 %collective-permute-start.8 = (bf16[2,32,64,128]{3,2,1,0:T(8,128)(2,1)}, bf16[2,32,64,128]{3,2,1,0:T(8,128)(2,1)}, u32[]{:S(2)}, u32[]{:S(2)}) collective-permute-start(bf16[2,32,64,128]{3,2,1,0:T(8,128)(2,1)} %get-tuple-element.136), channel_id=1, source_target_pairs={{0,3},{1,2},{2,1},{3,0},{4,7},{5,6},{6,5},{7,4},{8,11},{9,10},{10,... | collective-permute-start | bytes 3145736 | tf_op jit(solution)/shard_map/ppermute | solution.py:889
  437.1 94.2 %copy-start.6 = (f32[32,16]{1,0:T(8,128)S(1)}, f32[32,16]{1,0:T(8,128)}, u32[]{:S(2)}) copy-start(f32[32,16]{1,0:T(8,128)} %copy.75.out_ref) | copy-start | bytes 6148
  437.1 94.2 %copy-start.7 = (f32[32,16]{1,0:T(8,128)S(1)}, f32[32,16]{1,0:T(8,128)}, u32[]{:S(2)}) copy-start(f32[32,16]{1,0:T(8,128)} %copy.89) | copy-start | bytes 6148
  437.1 96.3 %copy-start.9 = (f32[16,128]{1,0:T(8,128)S(1)}, f32[16,128]{1,0:T(8,128)}, u32[]{:S(2)}) copy-start(f32[16,128]{1,0:T(8,128)} %proj_ref.1) | copy-start | bytes 24580
  437.1 96.3 %copy-start.10 = (f32[16,128]{1,0:T(8,128)S(1)}, f32[16,128]{1,0:T(8,128)}, u32[]{:S(2)}) copy-start(f32[16,128]{1,0:T(8,128)} %down_ref.1) | copy-start | bytes 24580
  437.1 96.3 %copy-start.15 = (f32[16,128]{1,0:T(8,128)S(1)}, f32[16,128]{1,0:T(8,128)}, u32[]{:S(2)}) copy-start(f32[16,128]{1,0:T(8,128)} %param.39) | copy-start | bytes 24580
  437.1 96.3 %copy-start.16 = (f32[16,128]{1,0:T(8,128)S(1)}, f32[16,128]{1,0:T(8,128)}, u32[]{:S(2)}) copy-start(f32[16,128]{1,0:T(8,128)} %param.33) | copy-start | bytes 24580
  437.1 96.2 %copy-start.17 = (f32[16,128]{1,0:T(8,128)S(1)}, f32[16,128]{1,0:T(8,128)}, u32[]{:S(2)}) copy-start(f32[16,128]{1,0:T(8,128)} %param.29) | copy-start | bytes 24580
  437.1 96.2 %copy-start.18 = (f32[16,128]{1,0:T(8,128)S(1)}, f32[16,128]{1,0:T(8,128)}, u32[]{:S(2)}) copy-start(f32[16,128]{1,0:T(8,128)} %param.35) | copy-start | bytes 24580
  561.1 22.4 %copy-start.11 = (f32[4,512]{1,0:T(4,128)S(1)}, f32[4,512]{1,0:T(4,128)}, u32[]{:S(2)}) copy-start(f32[4,512]{1,0:T(4,128)} %up_ref.1) | copy-start | bytes 24580
  561.2 22.4 %copy-start.19 = (f32[4,512]{1,0:T(4,128)S(1)}, f32[4,512]{1,0:T(4,128)}, u32[]{:S(2)}) copy-start(f32[4,512]{1,0:T(4,128)} %param.38) | copy-start | bytes 24580
  561.2 22.4 %copy-start.20 = (f32[4,512]{1,0:T(4,128)S(1)}, f32[4,512]{1,0:T(4,128)}, u32[]{:S(2)}) copy-start(f32[4,512]{1,0:T(4,128)} %param.32) | copy-start | bytes 24580
  561.2 23.0 %slice-start = ((f32[2048,4]{1,0:T(8,128)}), f32[2,4]{1,0:T(2,128)S(1)}, s32[]{:S(2)}) async-start(f32[2048,4]{1,0:T(8,128)} %copy-done.4), calls=%async_computation | async-start | bytes 2048 | tf_op jit(solution)/shard_map/slice | solution.py:906
  561.2 22.9 %copy-start.12 = (f32[4,4]{1,0:T(4,128)S(1)}, f32[4,4]{1,0:T(4,128)}, u32[]{:S(2)}) copy-start(f32[4,4]{1,0:T(4,128)} %gains_ref.1) | copy-start | bytes 196
  561.2 22.9 %copy-start.21 = (f32[4,4]{1,0:T(4,128)S(1)}, f32[4,4]{1,0:T(4,128)}, u32[]{:S(2)}) copy-start(f32[4,4]{1,0:T(4,128)} %param.40) | copy-start | bytes 196
  561.2 22.9 %copy-start.22 = (f32[4,4]{1,0:T(4,128)S(1)}, f32[4,4]{1,0:T(4,128)}, u32[]{:S(2)}) copy-start(f32[4,4]{1,0:T(4,128)} %param.34) | copy-start | bytes 196
  561.2 23.5 %copy-start.23 = (f32[16,1]{0,1:T(1,128)S(1)}, f32[16,1]{0,1:T(1,128)}, u32[]{:S(2)}) copy-start(f32[16,1]{0,1:T(1,128)} %param.24) | copy-start | bytes 196
  561.2 23.5 %copy-start.24 = (f32[16,1]{0,1:T(1,128)S(1)}, f32[16,1]{0,1:T(1,128)}, u32[]{:S(2)}) copy-start(f32[16,1]{0,1:T(1,128)} %param.36) | copy-start | bytes 196
  561.3 23.5 %copy-start.25 = (f32[16,1]{0,1:T(1,128)S(1)}, f32[16,1]{0,1:T(1,128)}, u32[]{:S(2)}) copy-start(f32[16,1]{0,1:T(1,128)} %param.30) | copy-start | bytes 196
  (7 other events, 64.9 us)
